TPU v7x, 32 devices: a whole 2x2x4 slice. The times are simulated.
32 devices in a mesh: grp: 2 (over x), row: 16 (over z, y, core).
Axes of the slice: x: 2, y: 2, z: 4, core: 2. Of those that a mesh axis runs over, the one named last changes fastest.
Arguments:
- cell_coeffs: float32 [6, 32, 384], P(None, 'row'), may hold values from 0.5 to 2
- z_factor: float32 [4, 64, 384, 128], P(None, ('grp', 'row')), parts along dimension 1, may hold values from -0.022552745 to 0.022552745
- noise_cols: float32 [4, 64, 384, 128], P(None, ('grp', 'row')), parts along dimension 1, may hold values from -0.022552745 to 0.022552745
- q_bar: float32 [4, 64, 384, 256], P(None, ('grp', 'row')), parts along dimension 1, may hold values from -10 to 10
- r_bar: float32 [512, 256], P('grp'), parts along dimension 0, may hold values from -11.085125 to 11.085125
Outputs:
- z_grad: float32 [4, 64, 384, 128], P(None, ('grp', 'row')), parts along dimension 1
- noise_grad: float32 [4, 64, 384, 128], P(None, ('grp', 'row')), parts along dimension 1
There are 2 independent parts, one for each index of `grp`. A program takes and returns all parts, laid end to end along the dimension named above; an argument that names none is the same for every part. Nothing has to cross between parts.
All inputs are finite; a program needn't handle non-finite values.
Results may differ from a plain program's by a relative error of at most 0.000061.
Values sent between devices are 32-bit elements; how exact they have to be, the bound alone decides.
A program may use at most 64 MiB of HBM per device.

v0:
```python
import jax
import jax.numpy as jnp
from jax import lax
from jax.sharding import PartitionSpec as P

rate_scales = (0.4, 0.4, 0.1, 0.2, 0.1, 0.1)
exact = lax.Precision.HIGHEST


def padded(block, sides, width):
    for axis, dim in sides:
        count = lax.axis_size(axis)
        forward = [(i, i + 1) for i in range(count - 1)]
        backward = [(target, source) for source, target in forward]
        low = lax.ppermute(
            lax.slice_in_dim(block, block.shape[dim] - width, None, axis=dim), axis, forward
        )
        high = lax.ppermute(lax.slice_in_dim(block, 0, width, axis=dim), axis, backward)
        block = jnp.concatenate([low, block, high], axis=dim)
    return block


def local_part(values, scaled, transposed):
    detuning = scaled[0][..., None]
    mech_freq = scaled[1][..., None]
    coupling = scaled[2][..., None]
    cavity_loss = scaled[3][..., None]
    phonon_loss = scaled[4][..., None]
    light_x, light_p, motion_x, motion_p = (values[0], values[1], values[2], values[3])
    if transposed:
        return jnp.stack(
            [
                -0.5 * cavity_loss * light_x + detuning * light_p - 2.0 * coupling * motion_p,
                -detuning * light_x - 0.5 * cavity_loss * light_p,
                -2.0 * coupling * light_p - mech_freq * motion_p,
                mech_freq * motion_x - 0.5 * phonon_loss * motion_p,
            ]
        )
    return jnp.stack(
        [
            -0.5 * cavity_loss * light_x - detuning * light_p,
            detuning * light_x - 0.5 * cavity_loss * light_p - 2.0 * coupling * motion_x,
            mech_freq * motion_p,
            -mech_freq * motion_x - 0.5 * phonon_loss * motion_p - 2.0 * coupling * light_x,
        ]
    )


def hop_sources(values, scaled, transposed):
    hopping = scaled[5][..., None]
    if transposed:
        return jnp.stack([hopping * values[0], hopping * values[1]])
    return jnp.stack([values[1], values[0]])


def neighbours(source):
    middle = source[:, 1:-1]
    sideways = jnp.pad(middle, ((0, 0), (0, 0), (1, 1), (0, 0)))
    return source[:, :-2] + source[:, 2:] + sideways[:, :, :-2] + sideways[:, :, 2:]


def hop_add(local_term, hop_sums, scaled, transposed):
    hopping = scaled[5][..., None]
    if transposed:
        return jnp.stack(
            [local_term[0] + hop_sums[1], local_term[1] - hop_sums[0], local_term[2], local_term[3]]
        )
    return jnp.stack(
        [
            local_term[0] - hopping * hop_sums[0],
            local_term[1] + hopping * hop_sums[1],
            local_term[2],
            local_term[3],
        ]
    )


def rim_apply(values, scaled, transposed):
    source = hop_sources(values, scaled, transposed)
    extended = padded(source, (("row", 1),), 1)
    return hop_add(local_part(values, scaled, transposed), neighbours(extended), scaled, transposed)


def shallow_expand(values, scaled, transposed):
    first_term = rim_apply(values, scaled, transposed)
    second = rim_apply(first_term, scaled, transposed)
    return values + first_term + 0.5 * second


def on_device(cell_coeffs, z_factor, noise_cols, q_bar, r_bar):
    scaled = cell_coeffs * jnp.array(rate_scales, jnp.float32)[:, None, None]
    rank_cols = z_factor.shape[3]

    def expand(values, transposed):
        return shallow_expand(values, scaled, transposed)

    stacked = jnp.concatenate([expand(z_factor, False), noise_cols], axis=3)
    flat_rows = stacked.reshape(-1, stacked.shape[3])
    bar_rows = q_bar.reshape(-1, q_bar.shape[3])
    gram_matrix = lax.psum(jnp.einsum("ik,il->kl", flat_rows, flat_rows, precision=exact), "row")
    lower_factor = jnp.linalg.cholesky(gram_matrix)
    identity = jnp.eye(gram_matrix.shape[0], dtype=jnp.float32)
    r_inv = lax.linalg.triangular_solve(lower_factor, identity, left_side=True, lower=True).T
    upper_factor = lower_factor.T
    target = jnp.dot(upper_factor, jnp.triu(r_bar).T, precision=exact)
    q_fact = jnp.dot(flat_rows, r_inv, precision=exact)
    cross = lax.psum(jnp.einsum("ik,il->kl", bar_rows, q_fact, precision=exact), "row")
    middle = target - cross
    symmetric = jnp.tril(middle) + jnp.tril(middle, -1).T
    grad_rows = jnp.dot(
        bar_rows + jnp.dot(q_fact, symmetric, precision=exact), r_inv.T, precision=exact
    )
    grad_x = grad_rows.reshape(q_bar.shape)
    z_grad = expand(grad_x[..., :rank_cols], True)
    return (z_grad, grad_x[..., rank_cols:])


def solution(mesh):
    return jax.shard_map(
        on_device,
        mesh=mesh,
        in_specs=(
            P(None, "row", None),
            P(None, ("grp", "row"), None, None),
            P(None, ("grp", "row"), None, None),
            P(None, ("grp", "row"), None, None),
            P("grp", None),
        ),
        out_specs=(P(None, ("grp", "row"), None, None), P(None, ("grp", "row"), None, None)),
        check_vma=False,
    )
```

profile of v0, /device:TPU:9, one launch (start us, length us, event | category | flops | bytes accessed | tf_op | source)
XLA Modules:
  0.0 350.2 jit_solution(17974185893808140031)
XLA Ops:
  7.2 1.2 fusion.59
  8.5 3.7 %collective-permute-start = (f32[2,1,384,128]{3,2,1,0:T(8,128)S(1)}, f32[2,1,384,128]{3,2,1,0:T(8,128)S(1)}, u32[]{:S(2)}, u32[]{:S(2)}) collective-permute-start(f32[2,1,384,128]{3,2,1,0:T(8,128)S(1)} %get-tuple-element.52), channel_id=1, source_target_pairs={{0,1},{1,2},{2,3},{3,4},{4,5},{5,6},{6,7},{7,8},{8,9},{9,10},{10,1... | collective-permute-start | bytes 1179656 | tf_op jit(solution)/shard_map/ppermute | solution.py:15
  12.2 1.9 collective-permute-start.1
  14.3 0.6 multiply_bitcast_fusion
  15.0 1.9 collective-permute-done
  16.9 5.8 %collective-permute-done.1 = f32[2,1,384,128]{3,2,1,0:T(8,128)S(1)} collective-permute-done((f32[2,1,384,128]{3,2,1,0:T(8,128)S(1)}, f32[2,1,384,128]{3,2,1,0:T(8,128)S(1)}, u32[]{:S(2)}, u32[]{:S(2)}) %collective-permute-start.1) | collective-permute-done | bytes 393248 | tf_op jit(solution)/shard_map/ppermute | solution.py:18
  23.4 0.9 fusion.18
  24.4 1.9 collective-permute-start.2
  26.3 2.4 collective-permute-start.3
  28.9 0.6 fusion.54
  29.5 1.8 collective-permute-done.2
  31.3 5.2 %collective-permute-done.3 = f32[2,1,384,128]{3,2,1,0:T(8,128)S(1)} collective-permute-done((f32[2,1,384,128]{3,2,1,0:T(8,128)}, f32[2,1,384,128]{3,2,1,0:T(8,128)S(1)}, u32[]{:S(2)}, u32[]{:S(2)}) %collective-permute-start.3) | collective-permute-done | bytes 393248 | tf_op jit(solution)/shard_map/ppermute | solution.py:18
  36.8 1.1 fusion.23
  38.7 1.1 copy-done.2
  39.8 6.0 %convolution_bitcast_fusion.1 = f32[256,256]{0,1:T(8,128)} fusion(f32[4,2,384,128]{3,2,1,0:T(8,128)S(1)} %copy-done.4, f32[4,2,384,128]{3,2,1,0:T(8,128)S(1)} %fusion.1), kind=kOutput, calls=%fused_computation.12 | convolution fusion | flops 2416705536 | bytes 3407872 | tf_op jit(solution)/shard_map/ik,il->kl/dot_general | solution.py:100
  46.1 3.2 pad_maximum_fusion
  49.3 84.6 %all-reduce.8.cloned.1.call-done = f32[256,256]{0,1:T(8,128)} async-done(((f32[256,256]{0,1:T(8,128)}), f32[256,256]{0,1:T(8,128)}) %all-reduce.8.cloned.1.call-update) | async-done | bytes 262160 | tf_op jit(solution)/shard_map/psum | solution.py:100
  133.9 1.1 copy.10
  135.0 1.0 fusion.27
  136.0 11.7 %cholesky.50 = f32[128,128]{1,0:T(8,128)S(1)} custom-call(f32[128,128]{1,0:T(8,128)S(1)} %cholesky.118), custom_call_target="Cholesky" | custom-call | tf_op jit(solution)/shard_map/jit(cholesky)/cholesky | solution.py:101
  147.7 9.8 %custom-call.14 = f32[1,128,128]{1,2,0:T(8,128)S(1)} custom-call(f32[1,128,128]{2,1,0:T(8,128)S(1)} %get-tuple-element.58), custom_call_target="InvertDiagBlocksLowerTriangular" | custom-call | tf_op jit(solution)/shard_map/jit(cholesky)/cholesky | solution.py:101
  158.1 11.7 %cholesky.105 = f32[128,128]{1,0:T(8,128)S(1)} custom-call(f32[128,128]{1,0:T(8,128)S(1)} %convolution_subtract_fusion.2), custom_call_target="Cholesky" | custom-call | tf_op jit(solution)/shard_map/jit(cholesky)/cholesky | solution.py:101
  169.8 0.7 compare_reduce_fusion
  172.0 5.3 %while.1 = (s32[]{:T(128)}, f32[256,256]{1,0:T(8,128)S(1)}, s32[2,2]{1,0:T(2,128)S(1)}, f32[2,128,128]{2,1,0:T(8,128)}, s32[]{:T(128)}) while((s32[]{:T(128)}, f32[256,256]{1,0:T(8,128)S(1)}, s32[2,2]{1,0:T(2,128)S(1)}, f32[2,128,128]{2,1,0:T(8,128)}, s32[]{:T(128)}) %tuple.56), condition=%wide.while_cond, body=%wide.while_body.sunk | while | flops 2 | bytes 132205 | solution.py:103
  172.0 0.6 fusion.70
  172.6 2.0 bitcast_dynamic-update-slice_fusion.2
  174.7 0.6 fusion.70
  175.3 2.1 bitcast_dynamic-update-slice_fusion.2
  177.3 20.7 %custom-call.15 = f32[2,128,128]{1,2,0:T(8,128)S(1)} custom-call(f32[2,128,128]{2,1,0:T(8,128)} %get-tuple-element.9), custom_call_target="InvertDiagBlocksLowerTriangular" | custom-call | tf_op jit(solution)/shard_map/triangular_solve | solution.py:103
  198.3 1.0 convolution_subtract_fusion.1
  199.7 4.7 %fusion.33 = f32[3072,256]{1,0:T(8,128)S(1)} fusion(f32[3072,256]{1,0:T(8,128)} %bitcast.73, f32[128,256]{1,0:T(8,128)S(1)} %fusion.44, f32[128,256]{1,0:T(8,128)S(1)} %fusion.40), kind=kOutput, calls=%fused_computation.106 | convolution fusion | flops 2415984640 | bytes 6553600 | tf_op jit(solution)/shard_map/dot_general | solution.py:106
  204.4 5.9 %convolution_bitcast_fusion = f32[256,256]{0,1:T(8,128)} fusion(f32[3072,256]{1,0:T(8,128)S(1)} %fusion.33, f32[3072,256]{1,0:T(8,128)S(1)} %bitcast.72), kind=kOutput, calls=%fused_computation.11 | convolution fusion | flops 2415919104 | bytes 6553600 | tf_op jit(solution)/shard_map/ik,il->kl/dot_general | solution.py:107
  210.8 88.9 %all-reduce.10.cloned.1.call-done = f32[256,256]{0,1:T(8,128)} async-done(((f32[256,256]{0,1:T(8,128)}), f32[256,256]{0,1:T(8,128)}) %all-reduce.10.cloned.1.call-update) | async-done | bytes 262160 | tf_op jit(solution)/shard_map/psum | solution.py:107
  299.7 1.6 convolution_subtract_fusion
  301.3 0.8 copy.15
  302.1 4.9 %convolution_add_fusion = f32[3072,256]{1,0:T(8,128)S(1)} fusion(f32[3072,256]{1,0:T(8,128)} %bitcast.71, f32[3072,256]{1,0:T(8,128)S(1)} %fusion.33, f32[256,256]{1,0:T(8,128)} %copy.15, f32[256,256]{0,1:T(8,128)S(1)} %convolution_subtract_fusion, s32[256]{0:T(256)} %iota_add_fusion), kind=kOutput, calls=%fused_computation.2 | convolution fusion | flops 2417033216 | bytes 9962496 | tf_op jit(solution)/shard_map/dot_general | solution.py:111
  307.0 2.9 fusion.32
  310.2 4.7 %collective-permute-start.4 = (f32[2,1,384,128]{3,2,1,0:T(8,128)S(1)}, f32[2,1,384,128]{3,2,1,0:T(8,128)S(1)}, u32[]{:S(2)}, u32[]{:S(2)}) collective-permute-start(f32[2,1,384,128]{3,2,1,0:T(8,128)S(1)} %get-tuple-element.48), channel_id=1, source_target_pairs={{0,1},{1,2},{2,3},{3,4},{4,5},{5,6},{6,7},{7,8},{8,9},{9,10},{10,1... | collective-permute-start | bytes 1179656 | tf_op jit(solution)/shard_map/ppermute | solution.py:15
  314.9 1.9 collective-permute-start.5
  316.9 2.7 collective-permute-done.4
  319.6 6.7 %collective-permute-done.5 = f32[2,1,384,128]{3,2,1,0:T(8,128)S(1)} collective-permute-done((f32[2,1,384,128]{3,2,1,0:T(8,128)S(1)}, f32[2,1,384,128]{3,2,1,0:T(8,128)S(1)}, u32[]{:S(2)}, u32[]{:S(2)}) %collective-permute-start.5) | collective-permute-done | bytes 393248 | tf_op jit(solution)/shard_map/ppermute | solution.py:18
  326.6 0.8 broadcast_multiply_fusion.1
  327.4 1.9 collective-permute-start.6
  329.3 2.4 collective-permute-start.7
  331.8 6.4 %collective-permute-done.6 = f32[2,1,384,128]{3,2,1,0:T(8,128)S(1)} collective-permute-done((f32[2,1,384,128]{3,2,1,0:T(8,128)S(1)}, f32[2,1,384,128]{3,2,1,0:T(8,128)S(1)}, u32[]{:S(2)}, u32[]{:S(2)}) %collective-permute-start.6) | collective-permute-done | bytes 393248 | tf_op jit(solution)/shard_map/ppermute | solution.py:15
  338.3 1.1 collective-permute-done.7
  339.6 0.9 slice_add_fusion.1
  340.9 2.1 fusion.58
  (78 shorter events, 5.5 us)
Async XLA Ops:
  7.2 7.0 %copy-start.19 = (f32[6]{0:T(128)S(1)}, f32[6]{0:T(128)}, u32[]{:S(2)}) copy-start(f32[6]{0:T(128)} %constant.100.clone) | copy-start | bytes 76
  7.2 7.0 %copy-start.17 = (f32[6,2,384]{2,1,0:T(2,128)S(1)}, f32[6,2,384]{2,1,0:T(2,128)}, u32[]{:S(2)}) copy-start(f32[6,2,384]{2,1,0:T(2,128)} %param.6) | copy-start | bytes 55300
  7.2 126.7 %all-reduce.8.cloned.1.call-start = ((), (), s32[]{:S(2)}) async-start(), calls=%async_computation | async-start | bytes 524288 | tf_op jit(solution)/shard_map/psum | solution.py:100
  8.5 8.4 %collective-permute-start = (f32[2,1,384,128]{3,2,1,0:T(8,128)S(1)}, f32[2,1,384,128]{3,2,1,0:T(8,128)S(1)}, u32[]{:S(2)}, u32[]{:S(2)}) collective-permute-start(f32[2,1,384,128]{3,2,1,0:T(8,128)S(1)} %get-tuple-element.52), channel_id=1, source_target_pairs={{0,1},{1,2},{2,3},{3,4},{4,5},{5,6},{6,7},{7,8},{8,9},{9,10},{10,1... | collective-permute-start | bytes 1179656 | tf_op jit(solution)/shard_map/ppermute | solution.py:15
  12.2 10.5 %collective-permute-start.1 = (f32[2,1,384,128]{3,2,1,0:T(8,128)S(1)}, f32[2,1,384,128]{3,2,1,0:T(8,128)S(1)}, u32[]{:S(2)}, u32[]{:S(2)}) collective-permute-start(f32[2,1,384,128]{3,2,1,0:T(8,128)S(1)} %get-tuple-element.53), channel_id=1, source_target_pairs={{1,0},{2,1},{3,2},{4,3},{5,4},{6,5},{7,6},{8,7},{9,8},{10,9},{11,1... | collective-permute-start | bytes 1179656 | tf_op jit(solution)/shard_map/ppermute | solution.py:18
  14.2 183.9 %copy-start.9 = (pred[256,256]{1,0:T(32,128)(4,1)}, pred[256,256]{1,0:T(32,128)(4,1)S(1)}, u32[]{:S(2)}) copy-start(pred[256,256]{1,0:T(32,128)(4,1)S(1)} %iota_compare_fusion.3) | copy-start | bytes 196612
  14.9 21.8 %copy-start.12 = (f32[2,384]{1,0:T(2,128)}, f32[2,384]{1,0:T(2,128)S(1)}, u32[]{:S(2)}) copy-start(f32[2,384]{1,0:T(2,128)S(1)} %get-tuple-element.64) | copy-start | bytes 9220
  14.9 21.8 %copy-start.14 = (f32[2,384]{1,0:T(2,128)}, f32[2,384]{1,0:T(2,128)S(1)}, u32[]{:S(2)}) copy-start(f32[2,384]{1,0:T(2,128)S(1)} %get-tuple-element.62) | copy-start | bytes 9220
  14.9 22.9 %copy-start.10 = (f32[2,384]{1,0:T(2,128)}, f32[2,384]{1,0:T(2,128)S(1)}, u32[]{:S(2)}) copy-start(f32[2,384]{1,0:T(2,128)S(1)} %get-tuple-element.61) | copy-start | bytes 9220
  15.0 7.9 %copy-start = (f32[4,2,384,128]{3,2,1,0:T(8,128)S(1)}, f32[4,2,384,128]{3,2,1,0:T(8,128)}, u32[]{:S(2)}) copy-start(f32[4,2,384,128]{3,2,1,0:T(8,128)} %param.7) | copy-start | bytes 4718596
  24.4 6.9 %collective-permute-start.2 = (f32[2,1,384,128]{3,2,1,0:T(8,128)}, f32[2,1,384,128]{3,2,1,0:T(8,128)S(1)}, u32[]{:S(2)}, u32[]{:S(2)}) collective-permute-start(f32[2,1,384,128]{3,2,1,0:T(8,128)} %get-tuple-element.50), channel_id=1, source_target_pairs={{0,1},{1,2},{2,3},{3,4},{4,5},{5,6},{6,7},{7,8},{8,9},{9,10},{10,1... | collective-permute-start | bytes 1179656 | tf_op jit(solution)/shard_map/ppermute | solution.py:15
  26.3 10.2 %collective-permute-start.3 = (f32[2,1,384,128]{3,2,1,0:T(8,128)}, f32[2,1,384,128]{3,2,1,0:T(8,128)S(1)}, u32[]{:S(2)}, u32[]{:S(2)}) collective-permute-start(f32[2,1,384,128]{3,2,1,0:T(8,128)} %get-tuple-element.51), channel_id=1, source_target_pairs={{1,0},{2,1},{3,2},{4,3},{5,4},{6,5},{7,6},{8,7},{9,8},{10,9},{11,1... | collective-permute-start | bytes 1179656 | tf_op jit(solution)/shard_map/ppermute | solution.py:18
  28.9 143.0 %copy-start.8 = (pred[256,256]{1,0:T(32,128)(4,1)}, pred[256,256]{1,0:T(32,128)(4,1)S(1)}, u32[]{:S(2)}) copy-start(pred[256,256]{1,0:T(32,128)(4,1)S(1)} %copy.12) | copy-start | bytes 196612
  38.3 1.6 copy-start.4
  38.7 1.1 copy-start.2
  39.8 6.2 %copy-start.5 = (f32[4,2,384,128]{3,2,1,0:T(8,128)S(1)}, f32[4,2,384,128]{3,2,1,0:T(8,128)}, u32[]{:S(2)}) copy-start(f32[4,2,384,128]{3,2,1,0:T(8,128)} %param.8) | copy-start | bytes 4718596
  45.8 253.9 %all-reduce.10.cloned.1.call-start = ((), (), s32[]{:S(2)}) async-start(), calls=%async_computation.1 | async-start | bytes 524288 | tf_op jit(solution)/shard_map/psum | solution.py:107
  169.8 29.8 %copy-start.3 = (f32[256,256]{1,0:T(8,128)}, f32[256,256]{1,0:T(8,128)S(1)}, u32[]{:S(2)}) copy-start(f32[256,256]{1,0:T(8,128)S(1)} %get-tuple-element.56) | copy-start | bytes 786436
  199.7 4.7 %copy-start.6 = (f32[128,256]{1,0:T(8,128)}, f32[128,256]{1,0:T(8,128)S(1)}, u32[]{:S(2)}) copy-start(f32[128,256]{1,0:T(8,128)S(1)} %fusion.44) | copy-start | bytes 393220
  199.7 4.7 %copy-start.1 = (f32[4,2,384,256]{3,2,1,0:T(8,128)S(1)}, f32[4,2,384,256]{3,2,1,0:T(8,128)}, u32[]{:S(2)}) copy-start(f32[4,2,384,256]{3,2,1,0:T(8,128)} %param.9) | copy-start | bytes 9437188
  302.1 4.9 %copy-start.7 = (f32[128,256]{1,0:T(8,128)S(1)}, f32[128,256]{1,0:T(8,128)}, u32[]{:S(2)}) copy-start(f32[128,256]{1,0:T(8,128)} %copy-done.6) | copy-start | bytes 393220
  307.0 2.9 copy-start.13
  310.2 9.4 %collective-permute-start.4 = (f32[2,1,384,128]{3,2,1,0:T(8,128)S(1)}, f32[2,1,384,128]{3,2,1,0:T(8,128)S(1)}, u32[]{:S(2)}, u32[]{:S(2)}) collective-permute-start(f32[2,1,384,128]{3,2,1,0:T(8,128)S(1)} %get-tuple-element.48), channel_id=1, source_target_pairs={{0,1},{1,2},{2,3},{3,4},{4,5},{5,6},{6,7},{7,8},{8,9},{9,10},{10,1... | collective-permute-start | bytes 1179656 | tf_op jit(solution)/shard_map/ppermute | solution.py:15
  314.9 11.4 %collective-permute-start.5 = (f32[2,1,384,128]{3,2,1,0:T(8,128)S(1)}, f32[2,1,384,128]{3,2,1,0:T(8,128)S(1)}, u32[]{:S(2)}, u32[]{:S(2)}) collective-permute-start(f32[2,1,384,128]{3,2,1,0:T(8,128)S(1)} %get-tuple-element.49), channel_id=1, source_target_pairs={{1,0},{2,1},{3,2},{4,3},{5,4},{6,5},{7,6},{8,7},{9,8},{10,9},{11,1... | collective-permute-start | bytes 1179656 | tf_op jit(solution)/shard_map/ppermute | solution.py:18
  316.9 9.6 %copy-start.16 = (f32[2,384]{1,0:T(2,128)S(1)}, f32[2,384]{1,0:T(2,128)}, u32[]{:S(2)}) copy-start(f32[2,384]{1,0:T(2,128)} %get-tuple-element.67) | copy-start | bytes 9220
  327.4 10.8 %collective-permute-start.6 = (f32[2,1,384,128]{3,2,1,0:T(8,128)S(1)}, f32[2,1,384,128]{3,2,1,0:T(8,128)S(1)}, u32[]{:S(2)}, u32[]{:S(2)}) collective-permute-start(f32[2,1,384,128]{3,2,1,0:T(8,128)S(1)} %get-tuple-element.46), channel_id=1, source_target_pairs={{0,1},{1,2},{2,3},{3,4},{4,5},{5,6},{6,7},{7,8},{8,9},{9,10},{10,1... | collective-permute-start | bytes 1179656 | tf_op jit(solution)/shard_map/ppermute | solution.py:15
  329.3 10.0 %collective-permute-start.7 = (f32[2,1,384,128]{3,2,1,0:T(8,128)S(1)}, f32[2,1,384,128]{3,2,1,0:T(8,128)S(1)}, u32[]{:S(2)}, u32[]{:S(2)}) collective-permute-start(f32[2,1,384,128]{3,2,1,0:T(8,128)S(1)} %get-tuple-element.47), channel_id=1, source_target_pairs={{1,0},{2,1},{3,2},{4,3},{5,4},{6,5},{7,6},{8,7},{9,8},{10,9},{11,1... | collective-permute-start | bytes 1179656 | tf_op jit(solution)/shard_map/ppermute | solution.py:18
  331.8 7.7 %copy-start.11 = (f32[2,384]{1,0:T(2,128)S(1)}, f32[2,384]{1,0:T(2,128)}, u32[]{:S(2)}) copy-start(f32[2,384]{1,0:T(2,128)} %copy-done.10) | copy-start | bytes 9220
  331.8 7.7 %copy-start.15 = (f32[2,384]{1,0:T(2,128)S(1)}, f32[2,384]{1,0:T(2,128)}, u32[]{:S(2)}) copy-start(f32[2,384]{1,0:T(2,128)} %copy-done.14) | copy-start | bytes 9220
  339.5 0.9 copy-start.18
Sparse Core Ops, SparseCore 0:
  46.0 87.8 all-reduce.7
  210.4 89.2 all-reduce.9
where the time goes:
time: 357 us; the launch traced here: 350 us
  waiting for transfers between devices  205 us (57%)
  other arithmetic  69.7 us (20%)
  matrix products  27.9 us (8%)
  starting transfers between devices  21.2 us (6%)
  between operations  16.4 us (5%)
  local copies, waits for them, and re-layouts  9.86 us (3%)
    psum x1, waiting for transfers between devices, on_device(): lax.psum(jnp.einsum('ik,il->kl', bar_rows, q_fact, precision=exact), 'row')  88.9 us
    psum x1, waiting for transfers between devices, on_device(): lax.psum(jnp.einsum('ik,il->kl', flat_rows, flat_rows, precision=exact),...  84.6 us
    another operation x6, other arithmetic, on_device(): lower_factor = jnp.linalg.cholesky(gram_matrix)  34 us
    another operation x4, other arithmetic, on_device(): lax.linalg.triangular_solve(lower_factor, identity, left_side=True, lower...  20.8 us
    ppermute x4, waiting for transfers between devices, padded(): lax.ppermute(lax.slice_in_dim(block, 0, width, axis=dim), axis, backward)  18.8 us
    ppermute x4, waiting for transfers between devices, padded(): lax.ppermute(lax.slice_in_dim(block, block.shape[dim] - width, None, axis...  12.8 us
    ppermute x4, starting transfers between devices, padded(): lax.ppermute(lax.slice_in_dim(block, block.shape[dim] - width, None, axis...  12.3 us
    ppermute x4, starting transfers between devices, padded(): lax.ppermute(lax.slice_in_dim(block, 0, width, axis=dim), axis, backward)  8.65 us
  transfers between devices with their start and end apart: 10, of which 10 were waited for; matrix products, arithmetic and copies ran while one was open for 2% of the time, Pallas kernels for 0%

commit v1 on v0

--- a/solution.py
+++ b/solution.py
@@ -1,6 +1,10 @@
+import functools
+
 import jax
 import jax.numpy as jnp
 from jax import lax
+from jax.experimental import pallas as pl
+from jax.experimental.pallas import tpu as pltpu
 from jax.sharding import PartitionSpec as P
 
 rate_scales = (0.4, 0.4, 0.1, 0.2, 0.1, 0.1)
@@ -87,6 +91,191 @@
     return values + first_term + 0.5 * second
 
 
+def sum_kernel(count, part_ref, out_ref, half_in, half_sum, quarter_in, quarter_sum, piece_in, full, send_sem, recv_sem, peer_send, peer_recv, back_send, back_recv):
+    rows = part_ref.shape[0]
+    peers = count // 4
+    half, quarter, piece = rows // 2, rows // 4, rows // count
+    me = lax.axis_index("row")
+    low, mid, top = lax.rem(me, 2), lax.rem(me // 2, 2), me // 4
+    pair = me + 1 - 2 * low
+    across = me + 2 - 4 * mid
+
+    def other(step):
+        return lax.rem(top + step, peers)
+
+    def device(step):
+        return {"row": other(step) * 4 + lax.rem(me, 4)}
+
+    barrier = pltpu.get_barrier_semaphore()
+    pl.semaphore_signal(barrier, inc=1, device_id={"row": pair}, device_id_type=pl.DeviceIdType.MESH)
+    pl.semaphore_signal(barrier, inc=1, device_id={"row": across}, device_id_type=pl.DeviceIdType.MESH)
+    for step in range(1, peers):
+        pl.semaphore_signal(barrier, inc=1, device_id=device(step), device_id_type=pl.DeviceIdType.MESH)
+    pl.semaphore_wait(barrier, peers + 1)
+
+    def swap(source, target, slot, where):
+        return pltpu.make_async_remote_copy(
+            src_ref=source,
+            dst_ref=target,
+            send_sem=send_sem.at[slot],
+            recv_sem=recv_sem.at[slot],
+            device_id={"row": where},
+            device_id_type=pl.DeviceIdType.MESH,
+        )
+
+    first = swap(part_ref.at[pl.ds(pl.multiple_of((1 - low) * half, 8), half)], half_in, 0, pair)
+    first.start()
+    first.wait()
+    half_sum[...] = part_ref[pl.ds(pl.multiple_of(low * half, 8), half)] + half_in[...]
+    second = swap(half_sum.at[pl.ds(pl.multiple_of((1 - mid) * quarter, 8), quarter)], quarter_in, 1, across)
+    second.start()
+    second.wait()
+    quarter_sum[...] = half_sum[pl.ds(pl.multiple_of(mid * quarter, 8), quarter)] + quarter_in[...]
+
+    outgoing = []
+    for step in range(1, peers):
+        copy = pltpu.make_async_remote_copy(
+            src_ref=quarter_sum.at[pl.ds(pl.multiple_of(other(step) * piece, 8), piece)],
+            dst_ref=piece_in.at[step],
+            send_sem=peer_send.at[step],
+            recv_sem=peer_recv.at[step],
+            device_id=device(step),
+            device_id_type=pl.DeviceIdType.MESH,
+        )
+        copy.start()
+        outgoing.append(copy)
+    total = quarter_sum[pl.ds(pl.multiple_of(top * piece, 8), piece)]
+    for step, copy in enumerate(outgoing, 1):
+        copy.wait()
+        total = total + piece_in[step]
+    base = low * half + mid * quarter
+    mine = pl.ds(pl.multiple_of(base + top * piece, 8), piece)
+    full[mine] = total
+    returning = []
+    for step in range(1, peers):
+        copy = pltpu.make_async_remote_copy(
+            src_ref=full.at[mine],
+            dst_ref=full.at[mine],
+            send_sem=back_send.at[step],
+            recv_sem=back_recv.at[step],
+            device_id=device(step),
+            device_id_type=pl.DeviceIdType.MESH,
+        )
+        copy.start()
+        returning.append(copy)
+    for copy in returning:
+        copy.wait()
+    own_quarter = full.at[pl.ds(pl.multiple_of(base, 8), quarter)]
+    third = swap(own_quarter, own_quarter, 2, across)
+    third.start()
+    third.wait()
+    own_half = full.at[pl.ds(pl.multiple_of(low * half, 8), half)]
+    fourth = swap(own_half, own_half, 3, pair)
+    fourth.start()
+    fourth.wait()
+    out_ref[...] = full[...]
+
+
+def device_sum(part):
+    count = lax.axis_size("row")
+    rows, cols = part.shape
+    peers = count // 4
+    return pl.pallas_call(
+        functools.partial(sum_kernel, count),
+        out_shape=jax.ShapeDtypeStruct(part.shape, jnp.float32),
+        in_specs=[pl.BlockSpec(memory_space=pltpu.VMEM)],
+        out_specs=pl.BlockSpec(memory_space=pltpu.VMEM),
+        scratch_shapes=[
+            pltpu.VMEM((rows // 2, cols), jnp.float32),
+            pltpu.VMEM((rows // 2, cols), jnp.float32),
+            pltpu.VMEM((rows // 4, cols), jnp.float32),
+            pltpu.VMEM((rows // 4, cols), jnp.float32),
+            pltpu.VMEM((peers, rows // count, cols), jnp.float32),
+            pltpu.VMEM((rows, cols), jnp.float32),
+            pltpu.SemaphoreType.DMA((4,)),
+            pltpu.SemaphoreType.DMA((4,)),
+            pltpu.SemaphoreType.DMA((peers,)),
+            pltpu.SemaphoreType.DMA((peers,)),
+            pltpu.SemaphoreType.DMA((peers,)),
+            pltpu.SemaphoreType.DMA((peers,)),
+        ],
+        compiler_params=pltpu.CompilerParams(collective_id=0, has_side_effects=True, vmem_limit_bytes=24 * 2**20),
+    )(part)
+
+
+tile = 32
+
+
+def tile_inverse(block):
+    shape = (tile, tile)
+    row_ids = lax.broadcasted_iota(jnp.int32, shape, 0)
+    col_ids = lax.broadcasted_iota(jnp.int32, shape, 1)
+    right = (row_ids == col_ids).astype(jnp.float32)
+    left = block
+    scale = jnp.zeros(shape, jnp.float32)
+    for start in range(0, tile, 8):
+        columns = [
+            jnp.broadcast_to(left[start:, start + k : start + k + 1], (tile - start, tile)) for k in range(8)
+        ]
+        below_left, below_right = left[start:], right[start:]
+        ids = row_ids[start:]
+        for j in range(8):
+            pivot = columns[j][j : j + 1]
+            factor = jnp.where(ids > start + j, columns[j] * (1.0 / pivot), 0.0)
+            scale = jnp.where(row_ids == start + j, lax.rsqrt(pivot), scale)
+            for k in range(j + 1, 8):
+                columns[k] = columns[k] - factor * columns[k][j : j + 1]
+            below_left = below_left - factor * below_left[j : j + 1]
+            below_right = below_right - factor * below_right[j : j + 1]
+        if start:
+            left = jnp.concatenate([left[:start], below_left], axis=0)
+            right = jnp.concatenate([right[:start], below_right], axis=0)
+        else:
+            left, right = below_left, below_right
+    return right * scale
+
+
+def mul(a, b, contract):
+    return lax.dot_general(a, b, ((contract[0:1], contract[1:2]), ((), ())), precision=exact, preferred_element_type=jnp.float32)
+
+
+def factor_kernel(gram_ref, cross_ref, bar_ref, inv_ref, mix_ref, work):
+    size = gram_ref.shape[0]
+    row_ids = lax.broadcasted_iota(jnp.int32, (size, size), 0)
+    col_ids = lax.broadcasted_iota(jnp.int32, (size, size), 1)
+    work[:, :size] = gram_ref[...]
+    work[:, size:] = (row_ids == col_ids).astype(jnp.float32)
+    for start in range(0, size, tile):
+        stop = start + tile
+        small = tile_inverse(work[start:stop, start:stop])
+        panel = mul(small, work[start:stop, :], (1, 0))
+        work[start:stop, :] = panel
+        if stop < size:
+            update = mul(panel[:, :size].T, panel, (1, 0))
+            work[stop:, :] = work[stop:, :] - update[stop:]
+    upper = jnp.where(row_ids <= col_ids, work[:, :size], 0.0)
+    inverse = jnp.where(row_ids >= col_ids, work[:, size:], 0.0)
+    inv_ref[...] = inverse
+    bar = jnp.where(row_ids <= col_ids, bar_ref[...], 0.0)
+    middle = mul(upper, bar, (1, 1)) - mul(cross_ref[...], inverse, (1, 1))
+    symmetric = jnp.where(row_ids >= col_ids, middle, middle.T)
+    mix_ref[...] = mul(inverse.T, mul(symmetric, inverse, (1, 0)), (1, 0))
+
+
+def factor(gram, cross, r_bar):
+    size = gram.shape[0]
+    shape = jax.ShapeDtypeStruct((size, size), jnp.float32)
+    whole = pl.BlockSpec(memory_space=pltpu.VMEM)
+    return pl.pallas_call(
+        factor_kernel,
+        out_shape=(shape, shape),
+        in_specs=[whole] * 3,
+        out_specs=(whole, whole),
+        scratch_shapes=[pltpu.VMEM((size, 2 * size), jnp.float32)],
+        compiler_params=pltpu.CompilerParams(vmem_limit_bytes=24 * 2**20),
+    )(gram, cross, r_bar)
+
+
 def on_device(cell_coeffs, z_factor, noise_cols, q_bar, r_bar):
     scaled = cell_coeffs * jnp.array(rate_scales, jnp.float32)[:, None, None]
     rank_cols = z_factor.shape[3]
@@ -97,19 +286,12 @@
     stacked = jnp.concatenate([expand(z_factor, False), noise_cols], axis=3)
     flat_rows = stacked.reshape(-1, stacked.shape[3])
     bar_rows = q_bar.reshape(-1, q_bar.shape[3])
-    gram_matrix = lax.psum(jnp.einsum("ik,il->kl", flat_rows, flat_rows, precision=exact), "row")
-    lower_factor = jnp.linalg.cholesky(gram_matrix)
-    identity = jnp.eye(gram_matrix.shape[0], dtype=jnp.float32)
-    r_inv = lax.linalg.triangular_solve(lower_factor, identity, left_side=True, lower=True).T
-    upper_factor = lower_factor.T
-    target = jnp.dot(upper_factor, jnp.triu(r_bar).T, precision=exact)
-    q_fact = jnp.dot(flat_rows, r_inv, precision=exact)
-    cross = lax.psum(jnp.einsum("ik,il->kl", bar_rows, q_fact, precision=exact), "row")
-    middle = target - cross
-    symmetric = jnp.tril(middle) + jnp.tril(middle, -1).T
-    grad_rows = jnp.dot(
-        bar_rows + jnp.dot(q_fact, symmetric, precision=exact), r_inv.T, precision=exact
-    )
+    both = jnp.concatenate([flat_rows, bar_rows], axis=1)
+    products = lax.dot_general(both, flat_rows, (((0,), (0,)), ((), ())), precision=lax.Precision.HIGH)
+    products = device_sum(products)
+    size = flat_rows.shape[1]
+    inverse, mix = factor(products[:size], products[size:], r_bar)
+    grad_rows = jnp.dot(bar_rows, inverse, precision=lax.Precision.HIGH) + jnp.dot(flat_rows, mix, precision=lax.Precision.HIGH)
     grad_x = grad_rows.reshape(q_bar.shape)
     z_grad = expand(grad_x[..., :rank_cols], True)
     return (z_grad, grad_x[..., rank_cols:])

time: 357 us -> 115 us (0.32); the launches traced: 350 us -> 114 us
  waiting for transfers between devices: 205 us -> 32.6 us
  other arithmetic: 69.7 us -> 8.04 us
  Pallas kernels: 0 us -> 36.3 us
  matrix products: 27.9 us -> 11.2 us
  between operations: 16.4 us -> 0.98 us
    psum x2 -> x0, waiting for transfers between devices: 173 us -> none  [the longest x1 88.9 us: on_device(): lax.psum(jnp.einsum('ik,il->kl', bar_rows, q_fact, precision=exact), 'row')]
    another operation x10 -> x0, other arithmetic: 54.8 us -> none  [the longest x6 34 us: on_device(): lower_factor = jnp.linalg.cholesky(gram_matrix)]
    pallas_call x0 -> x2, Pallas kernels: none -> 36.3 us  [the longest x1 22.8 us: device_sum(): pl.pallas_call(functools.partial(sum_kernel, count), out_shape=jax.ShapeD...]
    dot_general x6 -> x3, matrix products: 25.9 us -> 11.2 us  [the longest x1 5.29 us: on_device(): lax.dot_general(both, flat_rows, (((0,), (0,)), ((), ())), precision=lax....]
    another operation x10 -> x0, local copies, waits for them, and re-layouts: 5.55 us -> none
  transfers between devices with their start and end apart: 10 -> 8, of which waited for: 10 -> 8; matrix products, arithmetic and copies ran while one was open for 2% -> 0% of each run, Pallas kernels for 0% -> 0%
where the time goes in v1:
time: 115 us; the launch traced here: 114 us
  Pallas kernels  36.3 us (32%)
  waiting for transfers between devices  32.6 us (28%)
  starting transfers between devices  18.6 us (16%)
  matrix products  11.2 us (10%)
  other arithmetic  8.04 us (7%)
  local copies, waits for them, and re-layouts  6.44 us (6%)
    pallas_call x1, Pallas kernels, device_sum(): pl.pallas_call(functools.partial(sum_kernel, count), out_shape=jax.ShapeD...  22.8 us
    ppermute x4, waiting for transfers between devices, padded(): lax.ppermute(lax.slice_in_dim(block, 0, width, axis=dim), axis, backward)  19.1 us
    ppermute x4, waiting for transfers between devices, padded(): lax.ppermute(lax.slice_in_dim(block, block.shape[dim] - width, None, axis...  13.6 us
    pallas_call x1, Pallas kernels, factor(): pl.pallas_call(factor_kernel, out_shape=(shape, shape), in_specs=[whole]...  13.4 us
    ppermute x4, starting transfers between devices, padded(): lax.ppermute(lax.slice_in_dim(block, block.shape[dim] - width, None, axis...  9.56 us
    ppermute x4, starting transfers between devices, padded(): lax.ppermute(lax.slice_in_dim(block, 0, width, axis=dim), axis, backward)  9.05 us
    dot_general x1, matrix products, on_device(): lax.dot_general(both, flat_rows, (((0,), (0,)), ((), ())), precision=lax....  5.29 us
    dot_general x1, matrix products, on_device(): jnp.dot(bar_rows, inverse, precision=lax.Precision.HIGH)  4.42 us
  transfers between devices with their start and end apart: 8, of which 8 were waited for; matrix products, arithmetic and copies ran while one was open for 0% of the time, Pallas kernels for 0%

profile of v1, /device:TPU:9, one launch (start us, length us, event | category | flops | bytes accessed | tf_op | source)
XLA Modules:
  0.0 114.1 jit_solution(13388303554841300728)
XLA Ops:
  0.7 1.2 %fusion.38 = (f32[1,2,384,128]{3,2,1,0:T(8,128)S(1)}, f32[1,2,384,128]{3,2,1,0:T(8,128)S(1)}) fusion(f32[4,2,384,128]{3,2,1,0:T(8,128)} %param.7), kind=kLoop, calls=%fused_computation.108 | loop fusion | bytes 1572864 | tf_op jit(solution)/shard_map/slice | solution.py:33
  1.8 0.1 fusion.25
  1.9 3.7 %collective-permute-start = (f32[2,1,384,128]{3,2,1,0:T(8,128)S(1)}, f32[2,1,384,128]{3,2,1,0:T(8,128)S(1)}, u32[]{:S(2)}, u32[]{:S(2)}) collective-permute-start(f32[2,1,384,128]{3,2,1,0:T(8,128)S(1)} %get-tuple-element.38), channel_id=1, source_target_pairs={{0,1},{1,2},{2,3},{3,4},{4,5},{5,6},{6,7},{7,8},{8,9},{9,10},{10,1... | collective-permute-start | bytes 1179656 | tf_op jit(solution)/shard_map/ppermute | solution.py:19
  5.6 1.9 %collective-permute-start.1 = (f32[2,1,384,128]{3,2,1,0:T(8,128)S(1)}, f32[2,1,384,128]{3,2,1,0:T(8,128)S(1)}, u32[]{:S(2)}, u32[]{:S(2)}) collective-permute-start(f32[2,1,384,128]{3,2,1,0:T(8,128)S(1)} %get-tuple-element.39), channel_id=1, source_target_pairs={{1,0},{2,1},{3,2},{4,3},{5,4},{6,5},{7,6},{8,7},{9,8},{10,9},{11,1... | collective-permute-start | bytes 1179656 | tf_op jit(solution)/shard_map/ppermute | solution.py:22
  7.6 0.1 broadcast_multiply_fusion.3
  7.6 0.1 pad_maximum_fusion.1
  7.7 2.6 %collective-permute-done = f32[2,1,384,128]{3,2,1,0:T(8,128)S(1)} collective-permute-done((f32[2,1,384,128]{3,2,1,0:T(8,128)S(1)}, f32[2,1,384,128]{3,2,1,0:T(8,128)S(1)}, u32[]{:S(2)}, u32[]{:S(2)}) %collective-permute-start) | collective-permute-done | bytes 393248 | tf_op jit(solution)/shard_map/ppermute | solution.py:19
  10.3 5.8 %collective-permute-done.1 = f32[2,1,384,128]{3,2,1,0:T(8,128)S(1)} collective-permute-done((f32[2,1,384,128]{3,2,1,0:T(8,128)S(1)}, f32[2,1,384,128]{3,2,1,0:T(8,128)S(1)}, u32[]{:S(2)}, u32[]{:S(2)}) %collective-permute-start.1) | collective-permute-done | bytes 393248 | tf_op jit(solution)/shard_map/ppermute | solution.py:22
  16.1 0.2 fusion.18
  16.3 0.6 fusion.31
  16.9 0.1 fusion.23
  16.9 1.9 %collective-permute-start.2 = (f32[2,1,384,128]{3,2,1,0:T(8,128)S(1)}, f32[2,1,384,128]{3,2,1,0:T(8,128)S(1)}, u32[]{:S(2)}, u32[]{:S(2)}) collective-permute-start(f32[2,1,384,128]{3,2,1,0:T(8,128)S(1)} %get-tuple-element.36), channel_id=1, source_target_pairs={{0,1},{1,2},{2,3},{3,4},{4,5},{5,6},{6,7},{7,8},{8,9},{9,10},{10,1... | collective-permute-start | bytes 1179656 | tf_op jit(solution)/shard_map/ppermute | solution.py:19
  18.9 2.4 %collective-permute-start.3 = (f32[2,1,384,128]{3,2,1,0:T(8,128)S(1)}, f32[2,1,384,128]{3,2,1,0:T(8,128)S(1)}, u32[]{:S(2)}, u32[]{:S(2)}) collective-permute-start(f32[2,1,384,128]{3,2,1,0:T(8,128)S(1)} %get-tuple-element.37), channel_id=1, source_target_pairs={{1,0},{2,1},{3,2},{4,3},{5,4},{6,5},{7,6},{8,7},{9,8},{10,9},{11,1... | collective-permute-start | bytes 1179656 | tf_op jit(solution)/shard_map/ppermute | solution.py:22
  21.3 0.1 pad_maximum_fusion.2
  21.4 2.2 %collective-permute-done.2 = f32[2,1,384,128]{3,2,1,0:T(8,128)S(1)} collective-permute-done((f32[2,1,384,128]{3,2,1,0:T(8,128)S(1)}, f32[2,1,384,128]{3,2,1,0:T(8,128)S(1)}, u32[]{:S(2)}, u32[]{:S(2)}) %collective-permute-start.2) | collective-permute-done | bytes 393248 | tf_op jit(solution)/shard_map/ppermute | solution.py:19
  23.6 5.3 %collective-permute-done.3 = f32[2,1,384,128]{3,2,1,0:T(8,128)S(1)} collective-permute-done((f32[2,1,384,128]{3,2,1,0:T(8,128)S(1)}, f32[2,1,384,128]{3,2,1,0:T(8,128)S(1)}, u32[]{:S(2)}, u32[]{:S(2)}) %collective-permute-start.3) | collective-permute-done | bytes 393248 | tf_op jit(solution)/shard_map/ppermute | solution.py:22
  28.9 0.2 fusion.15
  29.0 1.1 fusion.28
  30.1 0.4 multiply_subtract_fusion.3
  30.5 0.2 fusion.6
  30.8 1.2 %copy-done.3 = f32[4,2,384,128]{3,2,1,0:T(8,128)S(1)} copy-done((f32[4,2,384,128]{3,2,1,0:T(8,128)S(1)}, f32[4,2,384,128]{3,2,1,0:T(8,128)}, u32[]{:S(2)}) %copy-start.3) | copy-done | bytes 1572888
  31.9 0.2 pad_maximum_fusion
  32.1 1.7 %copy-done.2 = f32[4,2,384,256]{3,2,1,0:T(8,128)S(1)} copy-done((f32[4,2,384,256]{3,2,1,0:T(8,128)S(1)}, f32[4,2,384,256]{3,2,1,0:T(8,128)}, u32[]{:S(2)}) %copy-start.2) | copy-done | bytes 3145752
  33.8 5.3 %fusion.part_ref = f32[512,256]{1,0:T(8,128)S(1)} fusion(f32[3072,256]{1,0:T(8,128)S(1)} %bitcast.37, f32[3072,256]{1,0:T(8,128)S(1)} %bitcast.39), kind=kOutput, calls=%fused_computation | convolution fusion | flops 2417491968 | bytes 6815744 | tf_op jit(solution)/shard_map/dot_general | solution.py:290
  39.1 22.8 %shard_map.77 = f32[512,256]{1,0:T(8,128)S(1)} custom-call(f32[512,256]{1,0:T(8,128)S(1)} %fusion.part_ref), custom_call_target="tpu_custom_call" | custom-call | tf_op jit(solution)/shard_map/pallas_call | solution.py:183
  62.0 13.4 %shard_map.78 = (f32[256,256]{1,0:T(8,128)S(1)}, f32[256,256]{1,0:T(8,128)S(1)}) custom-call(f32[256,256]{1,0:T(8,128)S(1)} %get-tuple-element.41.gram_ref, f32[256,256]{1,0:T(8,128)S(1)} %get-tuple-element.40.cross_ref, f32[256,256]{1,0:T(8,128)S(1)} %copy-done), custom_call_target="tpu_custom_call" | custom-call | tf_op jit(solution)/shard_map/pallas_call | solution.py:269
  75.5 1.5 %fusion.40 = f32[3072,256]{0,1:T(8,128)S(1)} fusion(f32[3072,256]{1,0:T(8,128)S(1)} %bitcast.38, f32[256,256]{1,0:T(8,128)S(1)} %get-tuple-element.5), kind=kOutput, calls=%fused_computation.110 | convolution fusion | flops 1207959552 | bytes 6553600 | tf_op jit(solution)/shard_map/dot_general | solution.py:294
  76.9 4.4 %fusion.4 = f32[3072,256]{0,1:T(8,128)} fusion(f32[3072,256]{0,1:T(8,128)S(1)} %fusion.40, f32[256,256]{1,0:T(8,128)S(1)} %get-tuple-element.4, f32[3072,256]{1,0:T(8,128)S(1)} %bitcast.40), kind=kOutput, calls=%fused_computation.5 | convolution fusion | flops 1208745984 | bytes 9699328 | tf_op jit(solution)/shard_map/dot_general | solution.py:294
  81.3 2.4 %copy.16 = f32[3072,256]{1,0:T(8,128)S(1)} copy(f32[3072,256]{0,1:T(8,128)} %fusion.4) | data formatting | bytes 6291456 | tf_op jit(solution)/shard_map/reshape | solution.py:295
  83.7 0.2 slice_multiply_fusion.7
  83.9 0.1 fusion.21
  84.0 2.0 %collective-permute-start.4 = (f32[2,1,384,128]{3,2,1,0:T(8,128)S(1)}, f32[2,1,384,128]{3,2,1,0:T(8,128)S(1)}, u32[]{:S(2)}, u32[]{:S(2)}) collective-permute-start(f32[2,1,384,128]{3,2,1,0:T(8,128)S(1)} %get-tuple-element.34), channel_id=1, source_target_pairs={{0,1},{1,2},{2,3},{3,4},{4,5},{5,6},{6,7},{7,8},{8,9},{9,10},{10,1... | collective-permute-start | bytes 1179656 | tf_op jit(solution)/shard_map/ppermute | solution.py:19
  86.0 2.3 %collective-permute-start.5 = (f32[2,1,384,128]{3,2,1,0:T(8,128)S(1)}, f32[2,1,384,128]{3,2,1,0:T(8,128)S(1)}, u32[]{:S(2)}, u32[]{:S(2)}) collective-permute-start(f32[2,1,384,128]{3,2,1,0:T(8,128)S(1)} %get-tuple-element.35), channel_id=1, source_target_pairs={{1,0},{2,1},{3,2},{4,3},{5,4},{6,5},{7,6},{8,7},{9,8},{10,9},{11,1... | collective-permute-start | bytes 1179656 | tf_op jit(solution)/shard_map/ppermute | solution.py:22
  88.3 0.1 pad_maximum_fusion.3
  88.4 2.3 %collective-permute-done.4 = f32[2,1,384,128]{3,2,1,0:T(8,128)S(1)} collective-permute-done((f32[2,1,384,128]{3,2,1,0:T(8,128)S(1)}, f32[2,1,384,128]{3,2,1,0:T(8,128)S(1)}, u32[]{:S(2)}, u32[]{:S(2)}) %collective-permute-start.4) | collective-permute-done | bytes 393248 | tf_op jit(solution)/shard_map/ppermute | solution.py:19
  90.7 6.9 %collective-permute-done.5 = f32[2,1,384,128]{3,2,1,0:T(8,128)S(1)} collective-permute-done((f32[2,1,384,128]{3,2,1,0:T(8,128)S(1)}, f32[2,1,384,128]{3,2,1,0:T(8,128)S(1)}, u32[]{:S(2)}, u32[]{:S(2)}) %collective-permute-start.5) | collective-permute-done | bytes 393248 | tf_op jit(solution)/shard_map/ppermute | solution.py:22
  97.6 0.2 fusion.12
  97.8 0.8 broadcast_multiply_fusion.1
  98.6 0.1 fusion.19
  98.7 1.9 %collective-permute-start.6 = (f32[2,1,384,128]{3,2,1,0:T(8,128)S(1)}, f32[2,1,384,128]{3,2,1,0:T(8,128)S(1)}, u32[]{:S(2)}, u32[]{:S(2)}) collective-permute-start(f32[2,1,384,128]{3,2,1,0:T(8,128)S(1)} %get-tuple-element.32), channel_id=1, source_target_pairs={{0,1},{1,2},{2,3},{3,4},{4,5},{5,6},{6,7},{7,8},{8,9},{9,10},{10,1... | collective-permute-start | bytes 1179656 | tf_op jit(solution)/shard_map/ppermute | solution.py:19
  100.6 2.4 %collective-permute-start.7 = (f32[2,1,384,128]{3,2,1,0:T(8,128)S(1)}, f32[2,1,384,128]{3,2,1,0:T(8,128)S(1)}, u32[]{:S(2)}, u32[]{:S(2)}) collective-permute-start(f32[2,1,384,128]{3,2,1,0:T(8,128)S(1)} %get-tuple-element.33), channel_id=1, source_target_pairs={{1,0},{2,1},{3,2},{4,3},{5,4},{6,5},{7,6},{8,7},{9,8},{10,9},{11,1... | collective-permute-start | bytes 1179656 | tf_op jit(solution)/shard_map/ppermute | solution.py:22
  103.0 0.1 pad_maximum_fusion.4
  103.1 6.4 %collective-permute-done.6 = f32[2,1,384,128]{3,2,1,0:T(8,128)S(1)} collective-permute-done((f32[2,1,384,128]{3,2,1,0:T(8,128)S(1)}, f32[2,1,384,128]{3,2,1,0:T(8,128)S(1)}, u32[]{:S(2)}, u32[]{:S(2)}) %collective-permute-start.6) | collective-permute-done | bytes 393248 | tf_op jit(solution)/shard_map/ppermute | solution.py:19
  109.5 1.1 collective-permute-done.7
  110.6 0.2 fusion.9
  110.8 0.9 slice_add_fusion.1
  111.7 0.4 multiply_subtract_fusion
  112.1 2.1 %fusion.37 = (f32[4,2,384,128]{3,2,1,0:T(8,128)}, f32[4,2,384,128]{3,2,1,0:T(8,128)}) fusion(f32[4,2,384,256]{3,2,1,0:T(8,128)S(1)} %bitcast.36, f32[1,2,384,128]{3,2,1,0:T(8,128)S(1)} %get-tuple-element.12, f32[1,2,384,128]{3,2,1,0:T(8,128)S(1)} %get-tuple-element.42, f32[1,2,384,128]{3,2,1,0:T(8,128)S(1)} %get-tuple-element.29, ...), kind=kLoop, calls=%fused_computation.107 | loop fusion | flops 3538944 | bytes 9437184 | tf_op jit(solution)/shard_map/slice | solution.py:297
  (13 shorter events, 0.1 us)
Async XLA Ops:
  0.6 6.9 %copy-start.5 = (f32[6]{0:T(128)S(1)}, f32[6]{0:T(128)}, u32[]{:S(2)}) copy-start(f32[6]{0:T(128)} %constant.14.clone) | copy-start | bytes 76
  0.6 6.9 %copy-start.4 = (f32[6,2,384]{2,1,0:T(2,128)S(1)}, f32[6,2,384]{2,1,0:T(2,128)}, u32[]{:S(2)}) copy-start(f32[6,2,384]{2,1,0:T(2,128)} %param.6) | copy-start | bytes 55300
  1.9 8.4 %collective-permute-start = (f32[2,1,384,128]{3,2,1,0:T(8,128)S(1)}, f32[2,1,384,128]{3,2,1,0:T(8,128)S(1)}, u32[]{:S(2)}, u32[]{:S(2)}) collective-permute-start(f32[2,1,384,128]{3,2,1,0:T(8,128)S(1)} %get-tuple-element.38), channel_id=1, source_target_pairs={{0,1},{1,2},{2,3},{3,4},{4,5},{5,6},{6,7},{7,8},{8,9},{9,10},{10,1... | collective-permute-start | bytes 1179656 | tf_op jit(solution)/shard_map/ppermute | solution.py:19
  5.6 10.5 %collective-permute-start.1 = (f32[2,1,384,128]{3,2,1,0:T(8,128)S(1)}, f32[2,1,384,128]{3,2,1,0:T(8,128)S(1)}, u32[]{:S(2)}, u32[]{:S(2)}) collective-permute-start(f32[2,1,384,128]{3,2,1,0:T(8,128)S(1)} %get-tuple-element.39), channel_id=1, source_target_pairs={{1,0},{2,1},{3,2},{4,3},{5,4},{6,5},{7,6},{8,7},{9,8},{10,9},{11,1... | collective-permute-start | bytes 1179656 | tf_op jit(solution)/shard_map/ppermute | solution.py:22
  7.7 8.6 %copy-start.1 = (f32[4,2,384,128]{3,2,1,0:T(8,128)S(1)}, f32[4,2,384,128]{3,2,1,0:T(8,128)}, u32[]{:S(2)}) copy-start(f32[4,2,384,128]{3,2,1,0:T(8,128)} %param.7) | copy-start | bytes 4718596
  16.9 6.6 %collective-permute-start.2 = (f32[2,1,384,128]{3,2,1,0:T(8,128)S(1)}, f32[2,1,384,128]{3,2,1,0:T(8,128)S(1)}, u32[]{:S(2)}, u32[]{:S(2)}) collective-permute-start(f32[2,1,384,128]{3,2,1,0:T(8,128)S(1)} %get-tuple-element.36), channel_id=1, source_target_pairs={{0,1},{1,2},{2,3},{3,4},{4,5},{5,6},{6,7},{7,8},{8,9},{9,10},{10,1... | collective-permute-start | bytes 1179656 | tf_op jit(solution)/shard_map/ppermute | solution.py:19
  18.9 10.0 %collective-permute-start.3 = (f32[2,1,384,128]{3,2,1,0:T(8,128)S(1)}, f32[2,1,384,128]{3,2,1,0:T(8,128)S(1)}, u32[]{:S(2)}, u32[]{:S(2)}) collective-permute-start(f32[2,1,384,128]{3,2,1,0:T(8,128)S(1)} %get-tuple-element.37), channel_id=1, source_target_pairs={{1,0},{2,1},{3,2},{4,3},{5,4},{6,5},{7,6},{8,7},{9,8},{10,9},{11,1... | collective-permute-start | bytes 1179656 | tf_op jit(solution)/shard_map/ppermute | solution.py:22
  30.5 1.4 %copy-start.3 = (f32[4,2,384,128]{3,2,1,0:T(8,128)S(1)}, f32[4,2,384,128]{3,2,1,0:T(8,128)}, u32[]{:S(2)}) copy-start(f32[4,2,384,128]{3,2,1,0:T(8,128)} %param.8) | copy-start | bytes 4718596
  31.9 1.9 %copy-start.2 = (f32[4,2,384,256]{3,2,1,0:T(8,128)S(1)}, f32[4,2,384,256]{3,2,1,0:T(8,128)}, u32[]{:S(2)}) copy-start(f32[4,2,384,256]{3,2,1,0:T(8,128)} %param.9) | copy-start | bytes 9437188
  39.1 22.9 %copy-start = (f32[256,256]{1,0:T(8,128)S(1)}, f32[256,256]{1,0:T(8,128)}, u32[]{:S(2)}) copy-start(f32[256,256]{1,0:T(8,128)} %bar_ref.1) | copy-start | bytes 786436
  84.0 6.7 %collective-permute-start.4 = (f32[2,1,384,128]{3,2,1,0:T(8,128)S(1)}, f32[2,1,384,128]{3,2,1,0:T(8,128)S(1)}, u32[]{:S(2)}, u32[]{:S(2)}) collective-permute-start(f32[2,1,384,128]{3,2,1,0:T(8,128)S(1)} %get-tuple-element.34), channel_id=1, source_target_pairs={{0,1},{1,2},{2,3},{3,4},{4,5},{5,6},{6,7},{7,8},{8,9},{9,10},{10,1... | collective-permute-start | bytes 1179656 | tf_op jit(solution)/shard_map/ppermute | solution.py:19
  86.0 11.6 %collective-permute-start.5 = (f32[2,1,384,128]{3,2,1,0:T(8,128)S(1)}, f32[2,1,384,128]{3,2,1,0:T(8,128)S(1)}, u32[]{:S(2)}, u32[]{:S(2)}) collective-permute-start(f32[2,1,384,128]{3,2,1,0:T(8,128)S(1)} %get-tuple-element.35), channel_id=1, source_target_pairs={{1,0},{2,1},{3,2},{4,3},{5,4},{6,5},{7,6},{8,7},{9,8},{10,9},{11,1... | collective-permute-start | bytes 1179656 | tf_op jit(solution)/shard_map/ppermute | solution.py:22
  98.7 10.8 %collective-permute-start.6 = (f32[2,1,384,128]{3,2,1,0:T(8,128)S(1)}, f32[2,1,384,128]{3,2,1,0:T(8,128)S(1)}, u32[]{:S(2)}, u32[]{:S(2)}) collective-permute-start(f32[2,1,384,128]{3,2,1,0:T(8,128)S(1)} %get-tuple-element.32), channel_id=1, source_target_pairs={{0,1},{1,2},{2,3},{3,4},{4,5},{5,6},{6,7},{7,8},{8,9},{9,10},{10,1... | collective-permute-start | bytes 1179656 | tf_op jit(solution)/shard_map/ppermute | solution.py:19
  100.6 10.0 %collective-permute-start.7 = (f32[2,1,384,128]{3,2,1,0:T(8,128)S(1)}, f32[2,1,384,128]{3,2,1,0:T(8,128)S(1)}, u32[]{:S(2)}, u32[]{:S(2)}) collective-permute-start(f32[2,1,384,128]{3,2,1,0:T(8,128)S(1)} %get-tuple-element.33), channel_id=1, source_target_pairs={{1,0},{2,1},{3,2},{4,3},{5,4},{6,5},{7,6},{8,7},{9,8},{10,9},{11,1... | collective-permute-start | bytes 1179656 | tf_op jit(solution)/shard_map/ppermute | solution.py:22

commit v2 on v1

--- a/solution.py
+++ b/solution.py
@@ -11,84 +11,196 @@
 exact = lax.Precision.HIGHEST
 
 
-def padded(block, sides, width):
-    for axis, dim in sides:
-        count = lax.axis_size(axis)
-        forward = [(i, i + 1) for i in range(count - 1)]
-        backward = [(target, source) for source, target in forward]
-        low = lax.ppermute(
-            lax.slice_in_dim(block, block.shape[dim] - width, None, axis=dim), axis, forward
+parts = 4
+margin = 8
+
+
+def step_kernel(count, transposed, coef_ref, value_ref, out_ref, coefs, first, source, source_two, send_low, recv_low, send_high, recv_high):
+    rows, cells, cols = value_ref.shape[1:]
+    chunk = cells // parts
+    me = lax.axis_index("row")
+    has_low, has_high = me > 0, me < count - 1
+
+    def link(buffer, stage, piece, upward):
+        cut = pl.ds(margin + piece * chunk, chunk)
+        sends, recvs = (send_high, recv_high) if upward else (send_low, recv_low)
+        slot = stage * parts + piece
+        return pltpu.make_async_remote_copy(
+            src_ref=buffer.at[:, rows if upward else 1, cut],
+            dst_ref=buffer.at[:, 0 if upward else rows + 1, cut],
+            send_sem=sends.at[slot],
+            recv_sem=recvs.at[slot],
+            device_id={"row": me + 1 if upward else me - 1},
+            device_id_type=pl.DeviceIdType.MESH,
         )
-        high = lax.ppermute(lax.slice_in_dim(block, 0, width, axis=dim), axis, backward)
-        block = jnp.concatenate([low, block, high], axis=dim)
-    return block
-
-
-def local_part(values, scaled, transposed):
-    detuning = scaled[0][..., None]
-    mech_freq = scaled[1][..., None]
-    coupling = scaled[2][..., None]
-    cavity_loss = scaled[3][..., None]
-    phonon_loss = scaled[4][..., None]
-    light_x, light_p, motion_x, motion_p = (values[0], values[1], values[2], values[3])
-    if transposed:
-        return jnp.stack(
-            [
-                -0.5 * cavity_loss * light_x + detuning * light_p - 2.0 * coupling * motion_p,
-                -detuning * light_x - 0.5 * cavity_loss * light_p,
-                -2.0 * coupling * light_p - mech_freq * motion_p,
-                mech_freq * motion_x - 0.5 * phonon_loss * motion_p,
-            ]
+
+    def send(buffer, stage, piece):
+        @pl.when(has_high)
+        def _():
+            link(buffer, stage, piece, True).start()
+
+        @pl.when(has_low)
+        def _():
+            link(buffer, stage, piece, False).start()
+
+    def receive(buffer, stage, piece):
+        @pl.when(has_low)
+        def _():
+            link(buffer, stage, piece, True).wait_recv()
+
+        @pl.when(has_high)
+        def _():
+            link(buffer, stage, piece, False).wait_recv()
+
+    barrier = pltpu.get_barrier_semaphore()
+
+    @pl.when(has_low)
+    def _():
+        pl.semaphore_signal(barrier, inc=1, device_id={"row": me - 1}, device_id_type=pl.DeviceIdType.MESH)
+
+    @pl.when(has_high)
+    def _():
+        pl.semaphore_signal(barrier, inc=1, device_id={"row": me + 1}, device_id_type=pl.DeviceIdType.MESH)
+
+    def coef(kind, row, piece):
+        return coefs[kind * rows + row, piece * chunk : (piece + 1) * chunk]
+
+    def at(piece):
+        return slice(piece * chunk, (piece + 1) * chunk)
+
+    def inner(piece, shift=0):
+        return slice(margin + piece * chunk + shift, margin + (piece + 1) * chunk + shift)
+
+    def spread(kind):
+        for row in range(rows):
+            index = kind * rows + row
+            coefs[index] = jnp.broadcast_to(coef_ref[:, index : index + 1], (cells, cols))
+
+    def fill(buffer, values, piece):
+        for row in range(rows):
+            for quad in range(2):
+                value = values[quad, row, at(piece)]
+                if transposed:
+                    value = value * coef(5, row, piece)
+                buffer[quad, row + 1, inner(piece)] = value
+
+    def zero_rim(buffer):
+        for quad in range(2):
+            for row in range(rows):
+                buffer[quad, row + 1, :margin] = jnp.zeros((margin, cols), jnp.float32)
+                buffer[quad, row + 1, margin + cells :] = jnp.zeros((margin, cols), jnp.float32)
+
+        @pl.when(jnp.logical_not(has_low))
+        def _():
+            buffer[:, 0] = jnp.zeros(buffer.shape[:1] + buffer.shape[2:], jnp.float32)
+
+        @pl.when(jnp.logical_not(has_high))
+        def _():
+            buffer[:, rows + 1] = jnp.zeros(buffer.shape[:1] + buffer.shape[2:], jnp.float32)
+
+    def local(values, buffer, row, piece):
+        xa, pa, xb, pb = [values[quad, row, at(piece)] for quad in range(4)]
+        detuning, mech, coupling, cavity, phonon, hopping = [coef(kind, row, piece) for kind in range(6)]
+        sums = []
+        for quad in range(2):
+            total = buffer[quad, row + 1, inner(piece, -1)] + buffer[quad, row + 1, inner(piece, 1)]
+            if row > 0:
+                total = total + buffer[quad, row, inner(piece)]
+            if row < rows - 1:
+                total = total + buffer[quad, row + 2, inner(piece)]
+            sums.append(total)
+        if transposed:
+            return (
+                -0.5 * cavity * xa + detuning * pa - 2.0 * coupling * pb + sums[1],
+                -detuning * xa - 0.5 * cavity * pa - sums[0],
+                -2.0 * coupling * pa - mech * pb,
+                mech * xb - 0.5 * phonon * pb,
+            )
+        return (
+            -0.5 * cavity * xa - detuning * pa - hopping * sums[1],
+            detuning * xa - 0.5 * cavity * pa - 2.0 * coupling * xb + hopping * sums[0],
+            mech * pb,
+            -mech * xb - 0.5 * phonon * pb - 2.0 * coupling * xa,
         )
-    return jnp.stack(
-        [
-            -0.5 * cavity_loss * light_x - detuning * light_p,
-            detuning * light_x - 0.5 * cavity_loss * light_p - 2.0 * coupling * motion_x,
-            mech_freq * motion_p,
-            -mech_freq * motion_x - 0.5 * phonon_loss * motion_p - 2.0 * coupling * light_x,
+
+    def edges(buffer, piece):
+        found = []
+        for row, halo in ((0, 0), (rows - 1, rows + 1)):
+            light_x, light_p = buffer[0, halo, inner(piece)], buffer[1, halo, inner(piece)]
+            if transposed:
+                found.append((row, light_p, -light_x))
+            else:
+                hopping = coef(5, row, piece)
+                found.append((row, -hopping * light_p, hopping * light_x))
+        return found
+
+    spread(5)
+    fill(source, value_ref, 0)
+
+    pl.semaphore_wait(barrier, jnp.where(me > 0, 1, 0) + jnp.where(me < count - 1, 1, 0))
+
+    send(source, 0, 0)
+    for piece in range(1, parts):
+        fill(source, value_ref, piece)
+        send(source, 0, piece)
+    zero_rim(source)
+    zero_rim(source_two)
+    for kind in range(5):
+        spread(kind)
+    for piece in range(parts):
+        for row in range(rows):
+            for quad, value in enumerate(local(value_ref, source, row, piece)):
+                first[quad, row, at(piece)] = value
+    for piece in range(parts):
+        receive(source, 0, piece)
+        for row, add_x, add_p in edges(source, piece):
+            first[0, row, at(piece)] = first[0, row, at(piece)] + add_x
+            first[1, row, at(piece)] = first[1, row, at(piece)] + add_p
+        fill(source_two, first, piece)
+        send(source_two, 1, piece)
+    for piece in range(parts):
+        for row in range(rows):
+            for quad, value in enumerate(local(first, source_two, row, piece)):
+                out_ref[quad, row, at(piece)] = (
+                    value_ref[quad, row, at(piece)] + first[quad, row, at(piece)] + 0.5 * value
+                )
+    for piece in range(parts):
+        receive(source_two, 1, piece)
+        for row, add_x, add_p in edges(source_two, piece):
+            out_ref[0, row, at(piece)] = out_ref[0, row, at(piece)] + 0.5 * add_x
+            out_ref[1, row, at(piece)] = out_ref[1, row, at(piece)] + 0.5 * add_p
+    for stage, buffer in enumerate((source, source_two)):
+        for piece in range(parts):
+
+            @pl.when(has_high)
+            def _():
+                link(buffer, stage, piece, True).wait_send()
+
+            @pl.when(has_low)
+            def _():
+                link(buffer, stage, piece, False).wait_send()
+
+
+def second_order(coef_columns, values, transposed):
+    count = lax.axis_size("row")
+    quads, rows, cells, cols = values.shape
+    whole = pl.BlockSpec(memory_space=pltpu.VMEM)
+    return pl.pallas_call(
+        functools.partial(step_kernel, count, transposed),
+        out_shape=jax.ShapeDtypeStruct(values.shape, jnp.float32),
+        in_specs=[whole] * 2,
+        out_specs=whole,
+        scratch_shapes=[
+            pltpu.VMEM((coef_columns.shape[1], cells, cols), jnp.float32),
+            pltpu.VMEM((quads, rows, cells, cols), jnp.float32),
+            pltpu.VMEM((2, rows + 2, cells + 2 * margin, cols), jnp.float32),
+            pltpu.VMEM((2, rows + 2, cells + 2 * margin, cols), jnp.float32),
         ]
-    )
-
-
-def hop_sources(values, scaled, transposed):
-    hopping = scaled[5][..., None]
-    if transposed:
-        return jnp.stack([hopping * values[0], hopping * values[1]])
-    return jnp.stack([values[1], values[0]])
-
-
-def neighbours(source):
-    middle = source[:, 1:-1]
-    sideways = jnp.pad(middle, ((0, 0), (0, 0), (1, 1), (0, 0)))
-    return source[:, :-2] + source[:, 2:] + sideways[:, :, :-2] + sideways[:, :, 2:]
-
-
-def hop_add(local_term, hop_sums, scaled, transposed):
-    hopping = scaled[5][..., None]
-    if transposed:
-        return jnp.stack(
-            [local_term[0] + hop_sums[1], local_term[1] - hop_sums[0], local_term[2], local_term[3]]
-        )
-    return jnp.stack(
-        [
-            local_term[0] - hopping * hop_sums[0],
-            local_term[1] + hopping * hop_sums[1],
-            local_term[2],
-            local_term[3],
-        ]
-    )
-
-
-def rim_apply(values, scaled, transposed):
-    source = hop_sources(values, scaled, transposed)
-    extended = padded(source, (("row", 1),), 1)
-    return hop_add(local_part(values, scaled, transposed), neighbours(extended), scaled, transposed)
-
-
-def shallow_expand(values, scaled, transposed):
-    first_term = rim_apply(values, scaled, transposed)
-    second = rim_apply(first_term, scaled, transposed)
-    return values + first_term + 0.5 * second
+        + [pltpu.SemaphoreType.DMA((2 * parts,))] * 4,
+        compiler_params=pltpu.CompilerParams(
+            collective_id=2 if transposed else 1, has_side_effects=True, vmem_limit_bytes=40 * 2**20
+        ),
+    )(coef_columns, values)
 
 
 def sum_kernel(count, part_ref, out_ref, half_in, half_sum, quarter_in, quarter_sum, piece_in, full, send_sem, recv_sem, peer_send, peer_recv, back_send, back_recv):
@@ -279,11 +391,9 @@
 def on_device(cell_coeffs, z_factor, noise_cols, q_bar, r_bar):
     scaled = cell_coeffs * jnp.array(rate_scales, jnp.float32)[:, None, None]
     rank_cols = z_factor.shape[3]
-
-    def expand(values, transposed):
-        return shallow_expand(values, scaled, transposed)
-
-    stacked = jnp.concatenate([expand(z_factor, False), noise_cols], axis=3)
+    coef_columns = scaled.reshape(-1, scaled.shape[2]).T
+
+    stacked = jnp.concatenate([second_order(coef_columns, z_factor, False), noise_cols], axis=3)
     flat_rows = stacked.reshape(-1, stacked.shape[3])
     bar_rows = q_bar.reshape(-1, q_bar.shape[3])
     both = jnp.concatenate([flat_rows, bar_rows], axis=1)
@@ -293,7 +403,7 @@
     inverse, mix = factor(products[:size], products[size:], r_bar)
     grad_rows = jnp.dot(bar_rows, inverse, precision=lax.Precision.HIGH) + jnp.dot(flat_rows, mix, precision=lax.Precision.HIGH)
     grad_x = grad_rows.reshape(q_bar.shape)
-    z_grad = expand(grad_x[..., :rank_cols], True)
+    z_grad = second_order(coef_columns, grad_x[..., :rank_cols], True)
     return (z_grad, grad_x[..., rank_cols:])
 
 

time: 115 us -> 98.8 us (0.86)
  Pallas kernels: 36.3 us -> 76.9 us
  waiting for transfers between devices: 32.6 us -> 0 us
  starting transfers between devices: 18.6 us -> 0 us
  other arithmetic: 8.04 us -> 1.01 us
  local copies, waits for them, and re-layouts: 6.44 us -> 8.27 us
    pallas_call x0 -> x2, Pallas kernels: none -> 40.6 us  [second_order(): pl.pallas_call(functools.partial(step_kernel, count, transposed), out_sha...]
    ppermute x8 -> x0, waiting for transfers between devices: 32.6 us -> none  [the longest x4 19.1 us: padded(): lax.ppermute(lax.slice_in_dim(block, 0, width, axis=dim), axis, backward)]
    ppermute x8 -> x0, starting transfers between devices: 18.6 us -> none  [the longest x4 9.56 us: padded(): lax.ppermute(lax.slice_in_dim(block, block.shape[dim] - width, None, axis...]
    add x7 -> x0, other arithmetic: 2.95 us -> none  [the longest x1 1.08 us: hop_add(): local_term[1] + hopping * hop_sums[1]]
    add x0 -> x1, local copies, waits for them, and re-layouts: none -> 2.37 us  [on_device(): jnp.dot(bar_rows, inverse, precision=lax.Precision.HIGH)]
    reshape x1 -> x2, local copies, waits for them, and re-layouts: 2.37 us -> 0.15 us  [on_device(): coef_columns = scaled.reshape(-1, scaled.shape[2]).T]
    slice x1 -> x0, other arithmetic: 2.08 us -> none  [on_device(): return (z_grad, grad_x[..., rank_cols:])]
    unnamed x12 -> x9, local copies, waits for them, and re-layouts: 2.85 us -> 4.23 us
  transfers between devices with their start and end apart: 8 -> 0, of which waited for: 8 -> 0; matrix products, arithmetic and copies ran while one was open for 0% -> 0% of each run, Pallas kernels for 0% -> 0%
where the time goes in v2:
time: 98.8 us; the launch traced here: 98.1 us
  Pallas kernels  76.9 us (78%)
  matrix products  11.2 us (11%)
  local copies, waits for them, and re-layouts  8.27 us (8%)
  other arithmetic  1.01 us (1%)
    pallas_call x2, Pallas kernels, second_order(): pl.pallas_call(functools.partial(step_kernel, count, transposed), out_sha...  40.6 us
    pallas_call x1, Pallas kernels, device_sum(): pl.pallas_call(functools.partial(sum_kernel, count), out_shape=jax.ShapeD...  22.8 us
    pallas_call x1, Pallas kernels, factor(): pl.pallas_call(factor_kernel, out_shape=(shape, shape), in_specs=[whole]...  13.5 us
    dot_general x1, matrix products, on_device(): lax.dot_general(both, flat_rows, (((0,), (0,)), ((), ())), precision=lax....  5.29 us
    dot_general x1, matrix products, on_device(): jnp.dot(bar_rows, inverse, precision=lax.Precision.HIGH)  4.44 us
    unnamed x9, local copies, waits for them, and re-layouts  4.23 us
    add x1, local copies, waits for them, and re-layouts, on_device(): jnp.dot(bar_rows, inverse, precision=lax.Precision.HIGH)  2.37 us

profile of v2, /device:TPU:9, one launch (start us, length us, event | category | flops | bytes accessed | tf_op | source)
XLA Modules:
  0.0 98.1 jit_solution(13560270201020465155)
XLA Ops:
  0.6 0.8 broadcast_multiply_fusion
  1.5 0.1 copy.11
  1.6 0.0 copy-start
  1.6 1.4 %copy-done = f32[4,2,384,128]{3,2,1,0:T(8,128)S(1)} copy-done((f32[4,2,384,128]{3,2,1,0:T(8,128)S(1)}, f32[4,2,384,128]{3,2,1,0:T(8,128)}, u32[]{:S(2)}) %copy-start) | copy-done | bytes 1572888
  3.0 0.0 copy-start.3
  3.0 20.4 %shard_map.77 = f32[4,2,384,128]{3,2,1,0:T(8,128)S(1)} custom-call(f32[384,12]{1,0:T(8,128)S(1)} %bitcast.13, f32[4,2,384,128]{3,2,1,0:T(8,128)S(1)} %copy-done), custom_call_target="tpu_custom_call" | custom-call | tf_op jit(solution)/shard_map/pallas_call | solution.py:188
  23.4 0.0 copy-done.3
  23.4 0.0 copy-start.2
  23.5 0.2 pad_maximum_fusion
  23.7 1.7 %copy-done.2 = f32[4,2,384,256]{3,2,1,0:T(8,128)S(1)} copy-done((f32[4,2,384,256]{3,2,1,0:T(8,128)S(1)}, f32[4,2,384,256]{3,2,1,0:T(8,128)}, u32[]{:S(2)}) %copy-start.2) | copy-done | bytes 3145752
  25.3 0.0 copy-start.1
  25.3 5.3 %fusion.part_ref = f32[512,256]{1,0:T(8,128)S(1)} fusion(f32[3072,256]{1,0:T(8,128)S(1)} %bitcast.15, f32[3072,256]{1,0:T(8,128)S(1)} %bitcast.18), kind=kOutput, calls=%fused_computation | convolution fusion | flops 2417491968 | bytes 6815744 | tf_op jit(solution)/shard_map/dot_general | solution.py:400
  30.6 22.8 %shard_map.78 = f32[512,256]{1,0:T(8,128)S(1)} custom-call(f32[512,256]{1,0:T(8,128)S(1)} %fusion.part_ref), custom_call_target="tpu_custom_call" | custom-call | tf_op jit(solution)/shard_map/pallas_call | solution.py:295
  53.5 0.0 copy-done.1
  53.5 13.5 %shard_map.79 = (f32[256,256]{1,0:T(8,128)S(1)}, f32[256,256]{1,0:T(8,128)S(1)}) custom-call(f32[256,256]{1,0:T(8,128)S(1)} %get-tuple-element.9.gram_ref, f32[256,256]{1,0:T(8,128)S(1)} %get-tuple-element.8.cross_ref, f32[256,256]{1,0:T(8,128)S(1)} %copy-done.1), custom_call_target="tpu_custom_call" | custom-call | tf_op jit(solution)/shard_map/pallas_call | solution.py:381
  67.0 1.5 %fusion.8 = f32[3072,256]{0,1:T(8,128)S(1)} fusion(f32[3072,256]{1,0:T(8,128)S(1)} %bitcast.16, f32[256,256]{1,0:T(8,128)S(1)} %get-tuple-element.5), kind=kOutput, calls=%fused_computation.11 | convolution fusion | flops 1207959552 | bytes 6553600 | tf_op jit(solution)/shard_map/dot_general | solution.py:404
  68.5 4.4 %fusion.4 = f32[3072,256]{0,1:T(8,128)} fusion(f32[3072,256]{0,1:T(8,128)S(1)} %fusion.8, f32[256,256]{1,0:T(8,128)S(1)} %get-tuple-element.4, f32[3072,256]{1,0:T(8,128)S(1)} %bitcast.19), kind=kOutput, calls=%fused_computation.5 | convolution fusion | flops 1208745984 | bytes 9699328 | tf_op jit(solution)/shard_map/dot_general | solution.py:404
  72.9 2.4 %copy.13 = f32[3072,256]{1,0:T(8,128)S(1)} copy(f32[3072,256]{0,1:T(8,128)} %fusion.4) | data formatting | bytes 6291456 | tf_op jit(solution)/shard_map/add | solution.py:404
  75.3 1.5 %fusion.6 = (f32[4,2,384,128]{3,2,1,0:T(8,128)}, f32[4,2,384,128]{3,2,1,0:T(8,128)S(1)}) fusion(f32[4,2,384,256]{3,2,1,0:T(8,128)S(1)} %bitcast.17), kind=kLoop, calls=%fused_computation.9 | loop fusion | bytes 6291456 | tf_op jit(solution)/shard_map/slice | solution.py:407
  76.8 20.2 %shard_map.80 = f32[4,2,384,128]{3,2,1,0:T(8,128)S(1)} custom-call(f32[384,12]{1,0:T(8,128)S(1)} %bitcast.14, f32[4,2,384,128]{3,2,1,0:T(8,128)S(1)} %get-tuple-element.7.value_ref), custom_call_target="tpu_custom_call" | custom-call | tf_op jit(solution)/shard_map/pallas_call | solution.py:188
  97.0 1.1 %copy.16 = f32[4,2,384,128]{3,2,1,0:T(8,128)} copy(f32[4,2,384,128]{3,2,1,0:T(8,128)S(1)} %shard_map.80) | data formatting | bytes 3145728
  (2 shorter events, 0.1 us)
Async XLA Ops:
  1.6 1.4 %copy-start = (f32[4,2,384,128]{3,2,1,0:T(8,128)S(1)}, f32[4,2,384,128]{3,2,1,0:T(8,128)}, u32[]{:S(2)}) copy-start(f32[4,2,384,128]{3,2,1,0:T(8,128)} %value_ref.1) | copy-start | bytes 4718596
  3.0 20.4 %copy-start.3 = (f32[4,2,384,128]{3,2,1,0:T(8,128)S(1)}, f32[4,2,384,128]{3,2,1,0:T(8,128)}, u32[]{:S(2)}) copy-start(f32[4,2,384,128]{3,2,1,0:T(8,128)} %param.8) | copy-start | bytes 4718596
  23.4 1.9 %copy-start.2 = (f32[4,2,384,256]{3,2,1,0:T(8,128)S(1)}, f32[4,2,384,256]{3,2,1,0:T(8,128)}, u32[]{:S(2)}) copy-start(f32[4,2,384,256]{3,2,1,0:T(8,128)} %param.9) | copy-start | bytes 9437188
  25.3 28.2 %copy-start.1 = (f32[256,256]{1,0:T(8,128)S(1)}, f32[256,256]{1,0:T(8,128)}, u32[]{:S(2)}) copy-start(f32[256,256]{1,0:T(8,128)} %bar_ref.1) | copy-start | bytes 786436

commit v3 on v2

--- a/solution.py
+++ b/solution.py
@@ -203,7 +203,7 @@
     )(coef_columns, values)
 
 
-def sum_kernel(count, part_ref, out_ref, half_in, half_sum, quarter_in, quarter_sum, piece_in, full, send_sem, recv_sem, peer_send, peer_recv, back_send, back_recv):
+def reduction(count, part_ref, half_in, half_sum, quarter_in, quarter_sum, piece_in, full, send_sem, recv_sem, peer_send, peer_recv, back_send, back_recv):
     rows = part_ref.shape[0]
     peers = count // 4
     half, quarter, piece = rows // 2, rows // 4, rows // count
@@ -215,47 +215,44 @@
     def other(step):
         return lax.rem(top + step, peers)
 
-    def device(step):
-        return {"row": other(step) * 4 + lax.rem(me, 4)}
-
-    barrier = pltpu.get_barrier_semaphore()
-    pl.semaphore_signal(barrier, inc=1, device_id={"row": pair}, device_id_type=pl.DeviceIdType.MESH)
-    pl.semaphore_signal(barrier, inc=1, device_id={"row": across}, device_id_type=pl.DeviceIdType.MESH)
-    for step in range(1, peers):
-        pl.semaphore_signal(barrier, inc=1, device_id=device(step), device_id_type=pl.DeviceIdType.MESH)
-    pl.semaphore_wait(barrier, peers + 1)
-
-    def swap(source, target, slot, where):
+    def copy_to(source, target, sends, recvs, slot, where):
         return pltpu.make_async_remote_copy(
             src_ref=source,
             dst_ref=target,
-            send_sem=send_sem.at[slot],
-            recv_sem=recv_sem.at[slot],
+            send_sem=sends.at[slot],
+            recv_sem=recvs.at[slot],
             device_id={"row": where},
             device_id_type=pl.DeviceIdType.MESH,
         )
 
-    first = swap(part_ref.at[pl.ds(pl.multiple_of((1 - low) * half, 8), half)], half_in, 0, pair)
+    first = copy_to(
+        part_ref.at[pl.ds(pl.multiple_of((1 - low) * half, 8), half)], half_in, send_sem, recv_sem, 0, pair
+    )
     first.start()
+    yield
     first.wait()
     half_sum[...] = part_ref[pl.ds(pl.multiple_of(low * half, 8), half)] + half_in[...]
-    second = swap(half_sum.at[pl.ds(pl.multiple_of((1 - mid) * quarter, 8), quarter)], quarter_in, 1, across)
+    second = copy_to(
+        half_sum.at[pl.ds(pl.multiple_of((1 - mid) * quarter, 8), quarter)], quarter_in, send_sem, recv_sem, 1, across
+    )
     second.start()
+    yield
     second.wait()
     quarter_sum[...] = half_sum[pl.ds(pl.multiple_of(mid * quarter, 8), quarter)] + quarter_in[...]
-
-    outgoing = []
-    for step in range(1, peers):
-        copy = pltpu.make_async_remote_copy(
-            src_ref=quarter_sum.at[pl.ds(pl.multiple_of(other(step) * piece, 8), piece)],
-            dst_ref=piece_in.at[step],
-            send_sem=peer_send.at[step],
-            recv_sem=peer_recv.at[step],
-            device_id=device(step),
-            device_id_type=pl.DeviceIdType.MESH,
+    outgoing = [
+        copy_to(
+            quarter_sum.at[pl.ds(pl.multiple_of(other(step) * piece, 8), piece)],
+            piece_in.at[step],
+            peer_send,
+            peer_recv,
+            step,
+            other(step) * 4 + lax.rem(me, 4),
         )
+        for step in range(1, peers)
+    ]
+    for copy in outgoing:
         copy.start()
-        outgoing.append(copy)
+    yield
     total = quarter_sum[pl.ds(pl.multiple_of(top * piece, 8), piece)]
     for step, copy in enumerate(outgoing, 1):
         copy.wait()
@@ -263,56 +260,39 @@
     base = low * half + mid * quarter
     mine = pl.ds(pl.multiple_of(base + top * piece, 8), piece)
     full[mine] = total
-    returning = []
-    for step in range(1, peers):
-        copy = pltpu.make_async_remote_copy(
-            src_ref=full.at[mine],
-            dst_ref=full.at[mine],
-            send_sem=back_send.at[step],
-            recv_sem=back_recv.at[step],
-            device_id=device(step),
-            device_id_type=pl.DeviceIdType.MESH,
-        )
+    returning = [
+        copy_to(full.at[mine], full.at[mine], back_send, back_recv, step, other(step) * 4 + lax.rem(me, 4))
+        for step in range(1, peers)
+    ]
+    for copy in returning:
         copy.start()
-        returning.append(copy)
+    yield
     for copy in returning:
         copy.wait()
     own_quarter = full.at[pl.ds(pl.multiple_of(base, 8), quarter)]
-    third = swap(own_quarter, own_quarter, 2, across)
+    third = copy_to(own_quarter, own_quarter, send_sem, recv_sem, 2, across)
     third.start()
+    yield
     third.wait()
     own_half = full.at[pl.ds(pl.multiple_of(low * half, 8), half)]
-    fourth = swap(own_half, own_half, 3, pair)
+    fourth = copy_to(own_half, own_half, send_sem, recv_sem, 3, pair)
     fourth.start()
+    yield
     fourth.wait()
-    out_ref[...] = full[...]
-
-
-def device_sum(part):
-    count = lax.axis_size("row")
-    rows, cols = part.shape
+
+
+def reduction_scratch(count, rows, cols):
     peers = count // 4
-    return pl.pallas_call(
-        functools.partial(sum_kernel, count),
-        out_shape=jax.ShapeDtypeStruct(part.shape, jnp.float32),
-        in_specs=[pl.BlockSpec(memory_space=pltpu.VMEM)],
-        out_specs=pl.BlockSpec(memory_space=pltpu.VMEM),
-        scratch_shapes=[
-            pltpu.VMEM((rows // 2, cols), jnp.float32),
-            pltpu.VMEM((rows // 2, cols), jnp.float32),
-            pltpu.VMEM((rows // 4, cols), jnp.float32),
-            pltpu.VMEM((rows // 4, cols), jnp.float32),
-            pltpu.VMEM((peers, rows // count, cols), jnp.float32),
-            pltpu.VMEM((rows, cols), jnp.float32),
-            pltpu.SemaphoreType.DMA((4,)),
-            pltpu.SemaphoreType.DMA((4,)),
-            pltpu.SemaphoreType.DMA((peers,)),
-            pltpu.SemaphoreType.DMA((peers,)),
-            pltpu.SemaphoreType.DMA((peers,)),
-            pltpu.SemaphoreType.DMA((peers,)),
-        ],
-        compiler_params=pltpu.CompilerParams(collective_id=0, has_side_effects=True, vmem_limit_bytes=24 * 2**20),
-    )(part)
+    return [
+        pltpu.VMEM((rows // 2, cols), jnp.float32),
+        pltpu.VMEM((rows // 2, cols), jnp.float32),
+        pltpu.VMEM((rows // 4, cols), jnp.float32),
+        pltpu.VMEM((rows // 4, cols), jnp.float32),
+        pltpu.VMEM((peers, rows // count, cols), jnp.float32),
+        pltpu.VMEM((rows, cols), jnp.float32),
+        pltpu.SemaphoreType.DMA((4,)),
+        pltpu.SemaphoreType.DMA((4,)),
+    ] + [pltpu.SemaphoreType.DMA((peers,))] * 4
 
 
 tile = 32
@@ -351,13 +331,48 @@
     return lax.dot_general(a, b, ((contract[0:1], contract[1:2]), ((), ())), precision=exact, preferred_element_type=jnp.float32)
 
 
-def factor_kernel(gram_ref, cross_ref, bar_ref, inv_ref, mix_ref, work):
-    size = gram_ref.shape[0]
+def factor_kernel(count, product_ref, bar_ref, inv_ref, mix_ref, work, gram_part, cross_part, *scratch):
+    size = bar_ref.shape[0]
+    side = size // 2
+    gram_scratch, cross_scratch = scratch[:12], scratch[12:]
+    gram_full, cross_full = gram_scratch[5], cross_scratch[5]
+    me = lax.axis_index("row")
+    low, mid, top = lax.rem(me, 2), lax.rem(me // 2, 2), me // 4
+    peers = count // 4
+    barrier = pltpu.get_barrier_semaphore()
+    friends = [me + 1 - 2 * low, me + 2 - 4 * mid]
+    friends += [lax.rem(top + step, peers) * 4 + lax.rem(me, 4) for step in range(1, peers)]
+    for friend in friends:
+        pl.semaphore_signal(barrier, inc=1, device_id={"row": friend}, device_id_type=pl.DeviceIdType.MESH)
+    gram_part[:side] = product_ref[:side, :side]
+    gram_part[side:size] = product_ref[side:size, :side]
+    gram_part[size : size + side] = product_ref[side:size, side:]
+    if gram_part.shape[0] > size + side:
+        gram_part[size + side :] = jnp.zeros((gram_part.shape[0] - size - side, side), jnp.float32)
+    cross_part[:size] = product_ref[size:, :side]
+    cross_part[size:] = product_ref[size:, side:]
+    pl.semaphore_wait(barrier, len(friends))
+    gram_steps = reduction(count, gram_part, *gram_scratch)
+    cross_steps = reduction(count, cross_part, *cross_scratch)
+    next(gram_steps)
+    next(gram_steps)
+    next(cross_steps)
+    next(gram_steps)
+    next(cross_steps)
+    next(gram_steps)
+    next(gram_steps)
+    next(gram_steps)
+    next(cross_steps)
+    next(gram_steps, None)
+
     row_ids = lax.broadcasted_iota(jnp.int32, (size, size), 0)
     col_ids = lax.broadcasted_iota(jnp.int32, (size, size), 1)
-    work[:, :size] = gram_ref[...]
+    work[:side, :side] = gram_full[:side]
+    work[side:, :side] = gram_full[side:size]
+    work[:side, side:size] = gram_full[side:size].T
+    work[side:, side:size] = gram_full[size : size + side]
     work[:, size:] = (row_ids == col_ids).astype(jnp.float32)
-    for start in range(0, size, tile):
+    for index, start in enumerate(range(0, size, tile)):
         stop = start + tile
         small = tile_inverse(work[start:stop, start:stop])
         panel = mul(small, work[start:stop, :], (1, 0))
@@ -365,27 +380,87 @@
         if stop < size:
             update = mul(panel[:, :size].T, panel, (1, 0))
             work[stop:, :] = work[stop:, :] - update[stop:]
+        if index in (1, 3, 5):
+            next(cross_steps)
     upper = jnp.where(row_ids <= col_ids, work[:, :size], 0.0)
     inverse = jnp.where(row_ids >= col_ids, work[:, size:], 0.0)
     inv_ref[...] = inverse
     bar = jnp.where(row_ids <= col_ids, bar_ref[...], 0.0)
-    middle = mul(upper, bar, (1, 1)) - mul(cross_ref[...], inverse, (1, 1))
+    target = mul(upper, bar, (1, 1))
+    next(cross_steps, None)
+    cross = jnp.concatenate([cross_full[:size], cross_full[size:]], axis=1)
+    middle = target - mul(cross, inverse, (1, 1))
     symmetric = jnp.where(row_ids >= col_ids, middle, middle.T)
     mix_ref[...] = mul(inverse.T, mul(symmetric, inverse, (1, 0)), (1, 0))
 
 
-def factor(gram, cross, r_bar):
-    size = gram.shape[0]
+def factor(products, r_bar):
+    count = lax.axis_size("row")
+    size = r_bar.shape[0]
+    side = size // 2
+    unit = 8 * count
+    gram_rows = (size + side + unit - 1) // unit * unit
     shape = jax.ShapeDtypeStruct((size, size), jnp.float32)
     whole = pl.BlockSpec(memory_space=pltpu.VMEM)
     return pl.pallas_call(
-        factor_kernel,
+        functools.partial(factor_kernel, count),
         out_shape=(shape, shape),
-        in_specs=[whole] * 3,
+        in_specs=[whole] * 2,
         out_specs=(whole, whole),
-        scratch_shapes=[pltpu.VMEM((size, 2 * size), jnp.float32)],
+        scratch_shapes=[
+            pltpu.VMEM((size, 2 * size), jnp.float32),
+            pltpu.VMEM((gram_rows, side), jnp.float32),
+            pltpu.VMEM((2 * size, side), jnp.float32),
+        ]
+        + reduction_scratch(count, gram_rows, side)
+        + reduction_scratch(count, 2 * size, side),
+        compiler_params=pltpu.CompilerParams(collective_id=0, has_side_effects=True, vmem_limit_bytes=24 * 2**20),
+    )(products, r_bar)
+
+
+def halves(value):
+    high = value.astype(jnp.bfloat16)
+    return high, (value - high.astype(jnp.float32)).astype(jnp.bfloat16)
+
+
+def three(left, high, low):
+    left_high, left_low = halves(left)
+    dot = functools.partial(jnp.dot, preferred_element_type=jnp.float32)
+    return dot(left_high, high) + (dot(left_high, low) + dot(left_low, high))
+
+
+def grad_kernel(bar_ref, z_ref, noise_ref, inv_ref, mix_ref, z_out, noise_out, inv_high, inv_low, mix_high, mix_low):
+    @pl.when(pl.program_id(0) == 0)
+    def _():
+        inv_high[...], inv_low[...] = halves(inv_ref[...])
+        mix_high[...], mix_low[...] = halves(mix_ref[...])
+
+    stacked = jnp.concatenate([z_ref[...], noise_ref[...]], axis=1)
+    grad = three(bar_ref[...], inv_high[...], inv_low[...]) + three(stacked, mix_high[...], mix_low[...])
+    z_out[...] = grad[:, : z_out.shape[1]]
+    noise_out[...] = grad[:, z_out.shape[1] :]
+
+
+def gradient(bar_rows, z_rows, noise_rows, inverse, mix):
+    rows, size = bar_rows.shape
+    block = rows // 8
+    square = pl.BlockSpec((size, size), lambda i: (0, 0))
+
+    def strip(value):
+        return pl.BlockSpec((block, value.shape[1]), lambda i: (i, 0))
+
+    return pl.pallas_call(
+        grad_kernel,
+        grid=(8,),
+        out_shape=(
+            jax.ShapeDtypeStruct(z_rows.shape, jnp.float32),
+            jax.ShapeDtypeStruct(noise_rows.shape, jnp.float32),
+        ),
+        in_specs=[strip(bar_rows), strip(z_rows), strip(noise_rows), square, square],
+        out_specs=(strip(z_rows), strip(noise_rows)),
+        scratch_shapes=[pltpu.VMEM((size, size), jnp.bfloat16)] * 4,
         compiler_params=pltpu.CompilerParams(vmem_limit_bytes=24 * 2**20),
-    )(gram, cross, r_bar)
+    )(bar_rows, z_rows, noise_rows, inverse, mix)
 
 
 def on_device(cell_coeffs, z_factor, noise_cols, q_bar, r_bar):
@@ -393,18 +468,16 @@
     rank_cols = z_factor.shape[3]
     coef_columns = scaled.reshape(-1, scaled.shape[2]).T
 
-    stacked = jnp.concatenate([second_order(coef_columns, z_factor, False), noise_cols], axis=3)
-    flat_rows = stacked.reshape(-1, stacked.shape[3])
+    z_rows = second_order(coef_columns, z_factor, False).reshape(-1, rank_cols)
+    noise_rows = noise_cols.reshape(-1, noise_cols.shape[3])
+    flat_rows = jnp.concatenate([z_rows, noise_rows], axis=1)
     bar_rows = q_bar.reshape(-1, q_bar.shape[3])
     both = jnp.concatenate([flat_rows, bar_rows], axis=1)
     products = lax.dot_general(both, flat_rows, (((0,), (0,)), ((), ())), precision=lax.Precision.HIGH)
-    products = device_sum(products)
-    size = flat_rows.shape[1]
-    inverse, mix = factor(products[:size], products[size:], r_bar)
-    grad_rows = jnp.dot(bar_rows, inverse, precision=lax.Precision.HIGH) + jnp.dot(flat_rows, mix, precision=lax.Precision.HIGH)
-    grad_x = grad_rows.reshape(q_bar.shape)
-    z_grad = second_order(coef_columns, grad_x[..., :rank_cols], True)
-    return (z_grad, grad_x[..., rank_cols:])
+    inverse, mix = factor(products, r_bar)
+    z_part, noise_part = gradient(bar_rows, z_rows, noise_rows, inverse, mix)
+    z_grad = second_order(coef_columns, z_part.reshape(z_factor.shape), True)
+    return (z_grad, noise_part.reshape(noise_cols.shape))
 
 
 def solution(mesh):

time: 98.8 us -> 97.4 us (0.986)
  Pallas kernels: 76.9 us -> 84.3 us
  local copies, waits for them, and re-layouts: 8.27 us -> 2.72 us
  matrix products: 11.2 us -> 7.16 us
    pallas_call x2, Pallas kernels: 36.3 us -> 43.3 us  [the longest x1 38.1 us: factor(): pl.pallas_call(functools.partial(factor_kernel, count), out_shape=(shape,...]
    dot_general x2 -> x0, matrix products: 5.89 us -> none  [the longest x1 4.44 us: on_device(): jnp.dot(bar_rows, inverse, precision=lax.Precision.HIGH)]
    add x1 -> x0, local copies, waits for them, and re-layouts: 2.37 us -> none  [on_device(): jnp.dot(bar_rows, inverse, precision=lax.Precision.HIGH)]
    dot_general x1, matrix products: 5.29 us -> 7.16 us  [on_device(): lax.dot_general(both, flat_rows, (((0,), (0,)), ((), ())), precision=lax....]
    unnamed x9, local copies, waits for them, and re-layouts: 4.23 us -> 2.57 us
    slice x2 -> x0, local copies, waits for them, and re-layouts: 1.52 us -> none  [the longest x1 1.49 us: on_device(): return (z_grad, grad_x[..., rank_cols:])]
where the time goes in v3:
time: 97.4 us; the launch traced here: 95.9 us
  Pallas kernels  84.3 us (87%)
  matrix products  7.16 us (7%)
  local copies, waits for them, and re-layouts  2.72 us (3%)
    pallas_call x2, Pallas kernels, second_order(): pl.pallas_call(functools.partial(step_kernel, count, transposed), out_sha...  41 us
    pallas_call x1, Pallas kernels, factor(): pl.pallas_call(functools.partial(factor_kernel, count), out_shape=(shape,...  38.1 us
    dot_general x1, matrix products, on_device(): lax.dot_general(both, flat_rows, (((0,), (0,)), ((), ())), precision=lax....  7.16 us
    pallas_call x1, Pallas kernels, gradient(): pl.pallas_call(grad_kernel, grid=(8,), out_shape=(jax.ShapeDtypeStruct(z_...  5.26 us
    unnamed x9, local copies, waits for them, and re-layouts  2.57 us

profile of v3, /device:TPU:9, one launch (start us, length us, event | category | flops | bytes accessed | tf_op | source)
XLA Modules:
  0.0 95.9 jit_solution(309159093773479458)
XLA Ops:
  0.6 0.0 copy-start
  0.6 1.0 broadcast_multiply_fusion
  1.6 0.1 copy.9
  1.8 0.0 copy-start.1
  1.8 1.4 %copy-done.1 = f32[4,2,384,128]{3,2,1,0:T(8,128)S(1)} copy-done((f32[4,2,384,128]{3,2,1,0:T(8,128)S(1)}, f32[4,2,384,128]{3,2,1,0:T(8,128)}, u32[]{:S(2)}) %copy-start.1) | copy-done | bytes 1572888
  3.2 20.4 %shard_map.77 = f32[4,2,384,128]{3,2,1,0:T(8,128)S(1)} custom-call(f32[384,12]{1,0:T(8,128)S(1)} %bitcast.10, f32[4,2,384,128]{3,2,1,0:T(8,128)S(1)} %copy-done.1), custom_call_target="tpu_custom_call" | custom-call | tf_op jit(solution)/shard_map/pallas_call | solution.py:188
  23.6 0.0 copy-done
  23.6 0.0 copy-start.3
  23.6 0.0 copy-start.2
  23.6 7.2 %fusion.product_ref = f32[512,256]{1,0:T(8,128)S(1)} fusion(f32[3072,256]{1,0:T(8,128)S(1)} %bitcast.8, f32[3072,128]{1,0:T(8,128)} %bitcast.13, f32[3072,128]{1,0:T(8,128)S(1)} %bitcast.6), kind=kOutput, calls=%fused_computation | convolution fusion | flops 2419851264 | bytes 6815744 | tf_op jit(solution)/shard_map/dot_general | solution.py:476
  30.8 0.0 copy-done.3
  30.8 38.1 %shard_map.78 = (f32[256,256]{1,0:T(8,128)S(1)}, f32[256,256]{1,0:T(8,128)S(1)}) custom-call(f32[512,256]{1,0:T(8,128)S(1)} %fusion.product_ref, f32[256,256]{1,0:T(8,128)S(1)} %copy-done.3), custom_call_target="tpu_custom_call" | custom-call | tf_op jit(solution)/shard_map/pallas_call | solution.py:405
  68.9 0.0 copy-done.2
  68.9 5.3 %shard_map.79 = (f32[3072,128]{1,0:T(8,128)S(1)}, f32[3072,128]{1,0:T(8,128)}) custom-call(f32[3072,256]{1,0:T(8,128)S(1)} %bitcast.9, f32[3072,128]{1,0:T(8,128)S(1)} %bitcast.7, f32[3072,128]{1,0:T(8,128)S(1)} %bitcast.14, f32[256,256]{1,0:T(8,128)S(1)} %get-tuple-element.6.inv_ref, f32[256,256]{1,0:T(8,128)S(1)} %get-tuple-element.7.mix_ref), custom_call_target="tpu_custom_call" | custom-call | tf_op jit(solution)/shard_map/pallas_call | solution.py:452
  74.2 20.6 %shard_map.80 = f32[4,2,384,128]{3,2,1,0:T(8,128)S(1)} custom-call(f32[384,12]{1,0:T(8,128)S(1)} %bitcast.11, f32[4,2,384,128]{3,2,1,0:T(8,128)S(1)} %bitcast.12), custom_call_target="tpu_custom_call" | custom-call | tf_op jit(solution)/shard_map/pallas_call | solution.py:188
  94.7 1.1 %copy.11 = f32[4,2,384,128]{3,2,1,0:T(8,128)} copy(f32[4,2,384,128]{3,2,1,0:T(8,128)S(1)} %shard_map.80) | data formatting | bytes 3145728
  (1 shorter events, 0.0 us)
Async XLA Ops:
  0.6 23.0 %copy-start = (f32[4,2,384,256]{3,2,1,0:T(8,128)S(1)}, f32[4,2,384,256]{3,2,1,0:T(8,128)}, u32[]{:S(2)}) copy-start(f32[4,2,384,256]{3,2,1,0:T(8,128)} %param.9) | copy-start | bytes 9437188
  1.8 1.4 %copy-start.1 = (f32[4,2,384,128]{3,2,1,0:T(8,128)S(1)}, f32[4,2,384,128]{3,2,1,0:T(8,128)}, u32[]{:S(2)}) copy-start(f32[4,2,384,128]{3,2,1,0:T(8,128)} %value_ref.1) | copy-start | bytes 4718596
  23.6 7.2 %copy-start.3 = (f32[256,256]{1,0:T(8,128)S(1)}, f32[256,256]{1,0:T(8,128)}, u32[]{:S(2)}) copy-start(f32[256,256]{1,0:T(8,128)} %bar_ref.1) | copy-start | bytes 786436
  23.6 45.3 %copy-start.2 = (f32[4,2,384,128]{3,2,1,0:T(8,128)S(1)}, f32[4,2,384,128]{3,2,1,0:T(8,128)}, u32[]{:S(2)}) copy-start(f32[4,2,384,128]{3,2,1,0:T(8,128)} %param.8) | copy-start | bytes 4718596

commit v4 on v3

--- a/solution.py
+++ b/solution.py
@@ -281,6 +281,51 @@
     fourth.wait()
 
 
+def direct_reduction(count, part_ref, piece_in, full, peer_send, peer_recv, back_send, back_recv):
+    piece = part_ref.shape[0] // count
+    me = lax.axis_index("row")
+    others = [lax.rem(me + step, count) for step in range(1, count)]
+    mine = pl.ds(pl.multiple_of(me * piece, 8), piece)
+
+    def copy_to(source, target, sends, recvs, step):
+        return pltpu.make_async_remote_copy(
+            src_ref=source,
+            dst_ref=target,
+            send_sem=sends.at[step],
+            recv_sem=recvs.at[step],
+            device_id={"row": others[step - 1]},
+            device_id_type=pl.DeviceIdType.MESH,
+        )
+
+    outgoing = [
+        copy_to(
+            part_ref.at[pl.ds(pl.multiple_of(other * piece, 8), piece)], piece_in.at[step], peer_send, peer_recv, step
+        )
+        for step, other in enumerate(others, 1)
+    ]
+    for copy in outgoing:
+        copy.start()
+    yield
+    total = part_ref[mine]
+    for step, copy in enumerate(outgoing, 1):
+        copy.wait()
+        total = total + piece_in[step]
+    full[mine] = total
+    returning = [copy_to(full.at[mine], full.at[mine], back_send, back_recv, step) for step in range(1, count)]
+    for copy in returning:
+        copy.start()
+    yield
+    for copy in returning:
+        copy.wait()
+
+
+def direct_scratch(count, rows, cols):
+    return [
+        pltpu.VMEM((count, rows // count, cols), jnp.float32),
+        pltpu.VMEM((rows, cols), jnp.float32),
+    ] + [pltpu.SemaphoreType.DMA((count,))] * 4
+
+
 def reduction_scratch(count, rows, cols):
     peers = count // 4
     return [
@@ -334,14 +379,11 @@
 def factor_kernel(count, product_ref, bar_ref, inv_ref, mix_ref, work, gram_part, cross_part, *scratch):
     size = bar_ref.shape[0]
     side = size // 2
-    gram_scratch, cross_scratch = scratch[:12], scratch[12:]
-    gram_full, cross_full = gram_scratch[5], cross_scratch[5]
+    gram_scratch, cross_scratch = scratch[:6], scratch[6:]
+    gram_full, cross_full = gram_scratch[1], cross_scratch[5]
     me = lax.axis_index("row")
-    low, mid, top = lax.rem(me, 2), lax.rem(me // 2, 2), me // 4
-    peers = count // 4
     barrier = pltpu.get_barrier_semaphore()
-    friends = [me + 1 - 2 * low, me + 2 - 4 * mid]
-    friends += [lax.rem(top + step, peers) * 4 + lax.rem(me, 4) for step in range(1, peers)]
+    friends = [lax.rem(me + step, count) for step in range(1, count)]
     for friend in friends:
         pl.semaphore_signal(barrier, inc=1, device_id={"row": friend}, device_id_type=pl.DeviceIdType.MESH)
     gram_part[:side] = product_ref[:side, :side]
@@ -352,18 +394,13 @@
     cross_part[:size] = product_ref[size:, :side]
     cross_part[size:] = product_ref[size:, side:]
     pl.semaphore_wait(barrier, len(friends))
-    gram_steps = reduction(count, gram_part, *gram_scratch)
+    gram_steps = direct_reduction(count, gram_part, *gram_scratch)
     cross_steps = reduction(count, cross_part, *cross_scratch)
-    next(gram_steps)
     next(gram_steps)
     next(cross_steps)
     next(gram_steps)
+    next(gram_steps, None)
     next(cross_steps)
-    next(gram_steps)
-    next(gram_steps)
-    next(gram_steps)
-    next(cross_steps)
-    next(gram_steps, None)
 
     row_ids = lax.broadcasted_iota(jnp.int32, (size, size), 0)
     col_ids = lax.broadcasted_iota(jnp.int32, (size, size), 1)
@@ -380,7 +417,7 @@
         if stop < size:
             update = mul(panel[:, :size].T, panel, (1, 0))
             work[stop:, :] = work[stop:, :] - update[stop:]
-        if index in (1, 3, 5):
+        if index in (1, 3, 4, 6):
             next(cross_steps)
     upper = jnp.where(row_ids <= col_ids, work[:, :size], 0.0)
     inverse = jnp.where(row_ids >= col_ids, work[:, size:], 0.0)
@@ -412,7 +449,7 @@
             pltpu.VMEM((gram_rows, side), jnp.float32),
             pltpu.VMEM((2 * size, side), jnp.float32),
         ]
-        + reduction_scratch(count, gram_rows, side)
+        + direct_scratch(count, gram_rows, side)
         + reduction_scratch(count, 2 * size, side),
         compiler_params=pltpu.CompilerParams(collective_id=0, has_side_effects=True, vmem_limit_bytes=24 * 2**20),
     )(products, r_bar)

time: 97.4 us -> 98.6 us (1.012)
  Pallas kernels: 84.3 us -> 86.3 us
    pallas_call x1, Pallas kernels: 38.1 us -> 40.4 us  [factor(): pl.pallas_call(functools.partial(factor_kernel, count), out_shape=(shape,...]
where the time goes in v4:
time: 98.6 us; the launch traced here: 97.8 us
  Pallas kernels  86.3 us (88%)
  matrix products  7.16 us (7%)
  local copies, waits for them, and re-layouts  2.72 us (3%)
    pallas_call x2, Pallas kernels, second_order(): pl.pallas_call(functools.partial(step_kernel, count, transposed), out_sha...  40.6 us
    pallas_call x1, Pallas kernels, factor(): pl.pallas_call(functools.partial(factor_kernel, count), out_shape=(shape,...  40.4 us
    dot_general x1, matrix products, on_device(): lax.dot_general(both, flat_rows, (((0,), (0,)), ((), ())), precision=lax....  7.16 us
    pallas_call x1, Pallas kernels, gradient(): pl.pallas_call(grad_kernel, grid=(8,), out_shape=(jax.ShapeDtypeStruct(z_...  5.26 us
    unnamed x9, local copies, waits for them, and re-layouts  2.57 us

profile of v4, /device:TPU:9, one launch (start us, length us, event | category | flops | bytes accessed | tf_op | source)
XLA Modules:
  0.0 97.8 jit_solution(12006022492890454115)
XLA Ops:
  0.6 0.0 copy-start
  0.6 1.0 broadcast_multiply_fusion
  1.6 0.1 copy.9
  1.8 0.0 copy-start.1
  1.8 1.4 %copy-done.1 = f32[4,2,384,128]{3,2,1,0:T(8,128)S(1)} copy-done((f32[4,2,384,128]{3,2,1,0:T(8,128)S(1)}, f32[4,2,384,128]{3,2,1,0:T(8,128)}, u32[]{:S(2)}) %copy-start.1) | copy-done | bytes 1572888
  3.2 20.4 %shard_map.77 = f32[4,2,384,128]{3,2,1,0:T(8,128)S(1)} custom-call(f32[384,12]{1,0:T(8,128)S(1)} %bitcast.10, f32[4,2,384,128]{3,2,1,0:T(8,128)S(1)} %copy-done.1), custom_call_target="tpu_custom_call" | custom-call | tf_op jit(solution)/shard_map/pallas_call | solution.py:188
  23.6 0.0 copy-done
  23.6 0.0 copy-start.3
  23.6 0.0 copy-start.2
  23.6 7.2 %fusion.product_ref = f32[512,256]{1,0:T(8,128)S(1)} fusion(f32[3072,256]{1,0:T(8,128)S(1)} %bitcast.8, f32[3072,128]{1,0:T(8,128)} %bitcast.13, f32[3072,128]{1,0:T(8,128)S(1)} %bitcast.6), kind=kOutput, calls=%fused_computation | convolution fusion | flops 2419851264 | bytes 6815744 | tf_op jit(solution)/shard_map/dot_general | solution.py:513
  30.8 0.0 copy-done.3
  30.8 40.4 %shard_map.78 = (f32[256,256]{1,0:T(8,128)S(1)}, f32[256,256]{1,0:T(8,128)S(1)}) custom-call(f32[512,256]{1,0:T(8,128)S(1)} %fusion.product_ref, f32[256,256]{1,0:T(8,128)S(1)} %copy-done.3), custom_call_target="tpu_custom_call" | custom-call | tf_op jit(solution)/shard_map/pallas_call | solution.py:442
  71.2 0.0 copy-done.2
  71.3 5.3 %shard_map.79 = (f32[3072,128]{1,0:T(8,128)S(1)}, f32[3072,128]{1,0:T(8,128)}) custom-call(f32[3072,256]{1,0:T(8,128)S(1)} %bitcast.9, f32[3072,128]{1,0:T(8,128)S(1)} %bitcast.7, f32[3072,128]{1,0:T(8,128)S(1)} %bitcast.14, f32[256,256]{1,0:T(8,128)S(1)} %get-tuple-element.6.inv_ref, f32[256,256]{1,0:T(8,128)S(1)} %get-tuple-element.7.mix_ref), custom_call_target="tpu_custom_call" | custom-call | tf_op jit(solution)/shard_map/pallas_call | solution.py:489
  76.5 20.2 %shard_map.80 = f32[4,2,384,128]{3,2,1,0:T(8,128)S(1)} custom-call(f32[384,12]{1,0:T(8,128)S(1)} %bitcast.11, f32[4,2,384,128]{3,2,1,0:T(8,128)S(1)} %bitcast.12), custom_call_target="tpu_custom_call" | custom-call | tf_op jit(solution)/shard_map/pallas_call | solution.py:188
  96.7 1.1 %copy.11 = f32[4,2,384,128]{3,2,1,0:T(8,128)} copy(f32[4,2,384,128]{3,2,1,0:T(8,128)S(1)} %shard_map.80) | data formatting | bytes 3145728
  (1 shorter events, 0.0 us)
Async XLA Ops:
  0.6 23.0 %copy-start = (f32[4,2,384,256]{3,2,1,0:T(8,128)S(1)}, f32[4,2,384,256]{3,2,1,0:T(8,128)}, u32[]{:S(2)}) copy-start(f32[4,2,384,256]{3,2,1,0:T(8,128)} %param.9) | copy-start | bytes 9437188
  1.8 1.4 %copy-start.1 = (f32[4,2,384,128]{3,2,1,0:T(8,128)S(1)}, f32[4,2,384,128]{3,2,1,0:T(8,128)}, u32[]{:S(2)}) copy-start(f32[4,2,384,128]{3,2,1,0:T(8,128)} %value_ref.1) | copy-start | bytes 4718596
  23.6 7.2 %copy-start.3 = (f32[256,256]{1,0:T(8,128)S(1)}, f32[256,256]{1,0:T(8,128)}, u32[]{:S(2)}) copy-start(f32[256,256]{1,0:T(8,128)} %bar_ref.1) | copy-start | bytes 786436
  23.6 47.6 %copy-start.2 = (f32[4,2,384,128]{3,2,1,0:T(8,128)S(1)}, f32[4,2,384,128]{3,2,1,0:T(8,128)}, u32[]{:S(2)}) copy-start(f32[4,2,384,128]{3,2,1,0:T(8,128)} %param.8) | copy-start | bytes 4718596

commit v5 on v3

--- a/solution.py
+++ b/solution.py
@@ -331,8 +331,8 @@
     return lax.dot_general(a, b, ((contract[0:1], contract[1:2]), ((), ())), precision=exact, preferred_element_type=jnp.float32)
 
 
-def factor_kernel(count, product_ref, bar_ref, inv_ref, mix_ref, work, gram_part, cross_part, *scratch):
-    size = bar_ref.shape[0]
+def sum_kernel(count, product_ref, gram_ref, cross_ref, gram_part, cross_part, *scratch):
+    size = gram_ref.shape[0]
     side = size // 2
     gram_scratch, cross_scratch = scratch[:12], scratch[12:]
     gram_full, cross_full = gram_scratch[5], cross_scratch[5]
@@ -354,25 +354,47 @@
     pl.semaphore_wait(barrier, len(friends))
     gram_steps = reduction(count, gram_part, *gram_scratch)
     cross_steps = reduction(count, cross_part, *cross_scratch)
-    next(gram_steps)
-    next(gram_steps)
-    next(cross_steps)
-    next(gram_steps)
-    next(cross_steps)
-    next(gram_steps)
-    next(gram_steps)
-    next(gram_steps)
-    next(cross_steps)
-    next(gram_steps, None)
-
+    for _ in range(7):
+        next(gram_steps, None)
+        next(cross_steps, None)
+    gram_ref[:side, :side] = gram_full[:side]
+    gram_ref[side:, :side] = gram_full[side:size]
+    gram_ref[:side, side:] = gram_full[side:size].T
+    gram_ref[side:, side:] = gram_full[size : size + side]
+    cross_ref[:, :side] = cross_full[:size]
+    cross_ref[:, side:] = cross_full[size:]
+
+
+def device_sum(products):
+    count = lax.axis_size("row")
+    size = products.shape[1]
+    side = size // 2
+    unit = 8 * count
+    gram_rows = (size + side + unit - 1) // unit * unit
+    shape = jax.ShapeDtypeStruct((size, size), jnp.float32)
+    whole = pl.BlockSpec(memory_space=pltpu.VMEM)
+    return pl.pallas_call(
+        functools.partial(sum_kernel, count),
+        out_shape=(shape, shape),
+        in_specs=[whole],
+        out_specs=(whole, whole),
+        scratch_shapes=[
+            pltpu.VMEM((gram_rows, side), jnp.float32),
+            pltpu.VMEM((2 * size, side), jnp.float32),
+        ]
+        + reduction_scratch(count, gram_rows, side)
+        + reduction_scratch(count, 2 * size, side),
+        compiler_params=pltpu.CompilerParams(collective_id=0, has_side_effects=True, vmem_limit_bytes=24 * 2**20),
+    )(products)
+
+
+def factor_kernel(gram_ref, cross_ref, bar_ref, inv_ref, mix_ref, work):
+    size = gram_ref.shape[0]
     row_ids = lax.broadcasted_iota(jnp.int32, (size, size), 0)
     col_ids = lax.broadcasted_iota(jnp.int32, (size, size), 1)
-    work[:side, :side] = gram_full[:side]
-    work[side:, :side] = gram_full[side:size]
-    work[:side, side:size] = gram_full[side:size].T
-    work[side:, side:size] = gram_full[size : size + side]
+    work[:, :size] = gram_ref[...]
     work[:, size:] = (row_ids == col_ids).astype(jnp.float32)
-    for index, start in enumerate(range(0, size, tile)):
+    for start in range(0, size, tile):
         stop = start + tile
         small = tile_inverse(work[start:stop, start:stop])
         panel = mul(small, work[start:stop, :], (1, 0))
@@ -380,42 +402,27 @@
         if stop < size:
             update = mul(panel[:, :size].T, panel, (1, 0))
             work[stop:, :] = work[stop:, :] - update[stop:]
-        if index in (1, 3, 5):
-            next(cross_steps)
     upper = jnp.where(row_ids <= col_ids, work[:, :size], 0.0)
     inverse = jnp.where(row_ids >= col_ids, work[:, size:], 0.0)
     inv_ref[...] = inverse
     bar = jnp.where(row_ids <= col_ids, bar_ref[...], 0.0)
-    target = mul(upper, bar, (1, 1))
-    next(cross_steps, None)
-    cross = jnp.concatenate([cross_full[:size], cross_full[size:]], axis=1)
-    middle = target - mul(cross, inverse, (1, 1))
+    middle = mul(upper, bar, (1, 1)) - mul(cross_ref[...], inverse, (1, 1))
     symmetric = jnp.where(row_ids >= col_ids, middle, middle.T)
     mix_ref[...] = mul(inverse.T, mul(symmetric, inverse, (1, 0)), (1, 0))
 
 
-def factor(products, r_bar):
-    count = lax.axis_size("row")
-    size = r_bar.shape[0]
-    side = size // 2
-    unit = 8 * count
-    gram_rows = (size + side + unit - 1) // unit * unit
+def factor(gram, cross, r_bar):
+    size = gram.shape[0]
     shape = jax.ShapeDtypeStruct((size, size), jnp.float32)
     whole = pl.BlockSpec(memory_space=pltpu.VMEM)
     return pl.pallas_call(
-        functools.partial(factor_kernel, count),
+        factor_kernel,
         out_shape=(shape, shape),
-        in_specs=[whole] * 2,
+        in_specs=[whole] * 3,
         out_specs=(whole, whole),
-        scratch_shapes=[
-            pltpu.VMEM((size, 2 * size), jnp.float32),
-            pltpu.VMEM((gram_rows, side), jnp.float32),
-            pltpu.VMEM((2 * size, side), jnp.float32),
-        ]
-        + reduction_scratch(count, gram_rows, side)
-        + reduction_scratch(count, 2 * size, side),
-        compiler_params=pltpu.CompilerParams(collective_id=0, has_side_effects=True, vmem_limit_bytes=24 * 2**20),
-    )(products, r_bar)
+        scratch_shapes=[pltpu.VMEM((size, 2 * size), jnp.float32)],
+        compiler_params=pltpu.CompilerParams(vmem_limit_bytes=24 * 2**20),
+    )(gram, cross, r_bar)
 
 
 def halves(value):
@@ -474,7 +481,8 @@
     bar_rows = q_bar.reshape(-1, q_bar.shape[3])
     both = jnp.concatenate([flat_rows, bar_rows], axis=1)
     products = lax.dot_general(both, flat_rows, (((0,), (0,)), ((), ())), precision=lax.Precision.HIGH)
-    inverse, mix = factor(products, r_bar)
+    gram, cross = device_sum(products)
+    inverse, mix = factor(gram, cross, r_bar)
     z_part, noise_part = gradient(bar_rows, z_rows, noise_rows, inverse, mix)
     z_grad = second_order(coef_columns, z_part.reshape(z_factor.shape), True)
     return (z_grad, noise_part.reshape(noise_cols.shape))

time: 97.4 us -> 92.6 us (0.951)
  Pallas kernels: 84.3 us -> 80.1 us
    pallas_call x1 -> x2, Pallas kernels: 38.1 us -> 34.3 us  [the longest x1 20.8 us: device_sum(): pl.pallas_call(functools.partial(sum_kernel, count), out_shape=(shape, sh...]
where the time goes in v5:
time: 92.6 us; the launch traced here: 91.7 us
  Pallas kernels  80.1 us (87%)
  matrix products  7.16 us (8%)
  local copies, waits for them, and re-layouts  2.72 us (3%)
  other arithmetic  0.95 us (1%)
    pallas_call x2, Pallas kernels, second_order(): pl.pallas_call(functools.partial(step_kernel, count, transposed), out_sha...  40.6 us
    pallas_call x1, Pallas kernels, device_sum(): pl.pallas_call(functools.partial(sum_kernel, count), out_shape=(shape, sh...  20.8 us
    pallas_call x1, Pallas kernels, factor(): pl.pallas_call(factor_kernel, out_shape=(shape, shape), in_specs=[whole]...  13.4 us
    dot_general x1, matrix products, on_device(): lax.dot_general(both, flat_rows, (((0,), (0,)), ((), ())), precision=lax....  7.16 us
    pallas_call x1, Pallas kernels, gradient(): pl.pallas_call(grad_kernel, grid=(8,), out_shape=(jax.ShapeDtypeStruct(z_...  5.26 us
    unnamed x9, local copies, waits for them, and re-layouts  2.57 us

profile of v5, /device:TPU:9, one launch (start us, length us, event | category | flops | bytes accessed | tf_op | source)
XLA Modules:
  0.0 91.7 jit_solution(10132652011664404558)
XLA Ops:
  0.6 0.0 copy-start
  0.6 1.0 %broadcast_multiply_fusion = f32[6,2,384]{2,1,0:T(2,128)S(1)} fusion(f32[6,2,384]{2,1,0:T(2,128)} %param.6, f32[6]{0:T(128)} %constant.2.clone), kind=kLoop, calls=%fused_computation.9 | loop fusion | flops 4608 | bytes 36888 | tf_op jit(solution)/shard_map/mul | solution.py:474
  1.6 0.1 copy.9
  1.8 0.0 copy-start.1
  1.8 1.4 %copy-done.1 = f32[4,2,384,128]{3,2,1,0:T(8,128)S(1)} copy-done((f32[4,2,384,128]{3,2,1,0:T(8,128)S(1)}, f32[4,2,384,128]{3,2,1,0:T(8,128)}, u32[]{:S(2)}) %copy-start.1) | copy-done | bytes 1572888
  3.2 20.4 %shard_map.77 = f32[4,2,384,128]{3,2,1,0:T(8,128)S(1)} custom-call(f32[384,12]{1,0:T(8,128)S(1)} %bitcast.10, f32[4,2,384,128]{3,2,1,0:T(8,128)S(1)} %copy-done.1), custom_call_target="tpu_custom_call" | custom-call | tf_op jit(solution)/shard_map/pallas_call | solution.py:188
  23.6 0.0 copy-done
  23.6 0.0 copy-start.3
  23.6 0.0 copy-start.2
  23.6 7.2 %fusion.product_ref = f32[512,256]{1,0:T(8,128)S(1)} fusion(f32[3072,256]{1,0:T(8,128)S(1)} %bitcast.8, f32[3072,128]{1,0:T(8,128)} %bitcast.13, f32[3072,128]{1,0:T(8,128)S(1)} %bitcast.6), kind=kOutput, calls=%fused_computation | convolution fusion | flops 2419851264 | bytes 6815744 | tf_op jit(solution)/shard_map/dot_general | solution.py:483
  30.8 20.8 %shard_map.78 = (f32[256,256]{1,0:T(8,128)S(1)}, f32[256,256]{1,0:T(8,128)S(1)}) custom-call(f32[512,256]{1,0:T(8,128)S(1)} %fusion.product_ref), custom_call_target="tpu_custom_call" | custom-call | tf_op jit(solution)/shard_map/pallas_call | solution.py:376
  51.6 0.0 copy-done.3
  51.7 13.4 %shard_map.79 = (f32[256,256]{1,0:T(8,128)S(1)}, f32[256,256]{1,0:T(8,128)S(1)}) custom-call(f32[256,256]{1,0:T(8,128)S(1)} %get-tuple-element.8.gram_ref, f32[256,256]{1,0:T(8,128)S(1)} %get-tuple-element.9.cross_ref, f32[256,256]{1,0:T(8,128)S(1)} %copy-done.3), custom_call_target="tpu_custom_call" | custom-call | tf_op jit(solution)/shard_map/pallas_call | solution.py:418
  65.1 0.0 copy-done.2
  65.1 5.3 %shard_map.80 = (f32[3072,128]{1,0:T(8,128)S(1)}, f32[3072,128]{1,0:T(8,128)}) custom-call(f32[3072,256]{1,0:T(8,128)S(1)} %bitcast.9, f32[3072,128]{1,0:T(8,128)S(1)} %bitcast.7, f32[3072,128]{1,0:T(8,128)S(1)} %bitcast.14, f32[256,256]{1,0:T(8,128)S(1)} %get-tuple-element.10.inv_ref, f32[256,256]{1,0:T(8,128)S(1)} %get-tuple-element.11.mix_ref), custom_call_target="tpu_custom_call" | custom-call | tf_op jit(solution)/shard_map/pallas_call | solution.py:459
  70.4 20.2 %shard_map.81 = f32[4,2,384,128]{3,2,1,0:T(8,128)S(1)} custom-call(f32[384,12]{1,0:T(8,128)S(1)} %bitcast.11, f32[4,2,384,128]{3,2,1,0:T(8,128)S(1)} %bitcast.12), custom_call_target="tpu_custom_call" | custom-call | tf_op jit(solution)/shard_map/pallas_call | solution.py:188
  90.6 1.1 %copy.11 = f32[4,2,384,128]{3,2,1,0:T(8,128)} copy(f32[4,2,384,128]{3,2,1,0:T(8,128)S(1)} %shard_map.81) | data formatting | bytes 3145728
  (1 shorter events, 0.0 us)
Async XLA Ops:
  0.6 23.0 %copy-start = (f32[4,2,384,256]{3,2,1,0:T(8,128)S(1)}, f32[4,2,384,256]{3,2,1,0:T(8,128)}, u32[]{:S(2)}) copy-start(f32[4,2,384,256]{3,2,1,0:T(8,128)} %param.9) | copy-start | bytes 9437188
  1.8 1.4 %copy-start.1 = (f32[4,2,384,128]{3,2,1,0:T(8,128)S(1)}, f32[4,2,384,128]{3,2,1,0:T(8,128)}, u32[]{:S(2)}) copy-start(f32[4,2,384,128]{3,2,1,0:T(8,128)} %value_ref.1) | copy-start | bytes 4718596
  23.6 28.0 %copy-start.3 = (f32[256,256]{1,0:T(8,128)S(1)}, f32[256,256]{1,0:T(8,128)}, u32[]{:S(2)}) copy-start(f32[256,256]{1,0:T(8,128)} %bar_ref.1) | copy-start | bytes 786436
  23.6 41.5 %copy-start.2 = (f32[4,2,384,128]{3,2,1,0:T(8,128)S(1)}, f32[4,2,384,128]{3,2,1,0:T(8,128)}, u32[]{:S(2)}) copy-start(f32[4,2,384,128]{3,2,1,0:T(8,128)} %param.8) | copy-start | bytes 4718596

commit v6 on v5

--- a/solution.py
+++ b/solution.py
@@ -400,8 +400,9 @@
         panel = mul(small, work[start:stop, :], (1, 0))
         work[start:stop, :] = panel
         if stop < size:
-            update = mul(panel[:, :size].T, panel, (1, 0))
-            work[stop:, :] = work[stop:, :] - update[stop:]
+            base, end = stop // 128 * 128, size + (stop + 127) // 128 * 128
+            update = mul(panel[:, base:size].T, panel[:, base:end], (1, 0))
+            work[stop:, base:end] = work[stop:, base:end] - update[stop - base :]
     upper = jnp.where(row_ids <= col_ids, work[:, :size], 0.0)
     inverse = jnp.where(row_ids >= col_ids, work[:, size:], 0.0)
     inv_ref[...] = inverse

time: 92.6 us -> 91.7 us (level)
    pallas_call x1, Pallas kernels: 13.4 us -> 12.5 us  [factor(): pl.pallas_call(factor_kernel, out_shape=(shape, shape), in_specs=[whole]...]
where the time goes in v6:
time: 91.7 us; the launch traced here: 90.8 us
  Pallas kernels  79.2 us (86%)
  matrix products  7.16 us (8%)
  local copies, waits for them, and re-layouts  2.72 us (3%)
  other arithmetic  0.95 us (1%)
    pallas_call x2, Pallas kernels, second_order(): pl.pallas_call(functools.partial(step_kernel, count, transposed), out_sha...  40.6 us
    pallas_call x1, Pallas kernels, device_sum(): pl.pallas_call(functools.partial(sum_kernel, count), out_shape=(shape, sh...  20.8 us
    pallas_call x1, Pallas kernels, factor(): pl.pallas_call(factor_kernel, out_shape=(shape, shape), in_specs=[whole]...  12.5 us
    dot_general x1, matrix products, on_device(): lax.dot_general(both, flat_rows, (((0,), (0,)), ((), ())), precision=lax....  7.16 us
    pallas_call x1, Pallas kernels, gradient(): pl.pallas_call(grad_kernel, grid=(8,), out_shape=(jax.ShapeDtypeStruct(z_...  5.27 us
    unnamed x9, local copies, waits for them, and re-layouts  2.57 us

profile of v6, /device:TPU:9, one launch (start us, length us, event | category | flops | bytes accessed | tf_op | source)
XLA Modules:
  0.0 90.8 jit_solution(1182639315638607438)
XLA Ops:
  0.6 0.0 copy-start
  0.6 1.0 %broadcast_multiply_fusion = f32[6,2,384]{2,1,0:T(2,128)S(1)} fusion(f32[6,2,384]{2,1,0:T(2,128)} %param.6, f32[6]{0:T(128)} %constant.2.clone), kind=kLoop, calls=%fused_computation.9 | loop fusion | flops 4608 | bytes 36888 | tf_op jit(solution)/shard_map/mul | solution.py:475
  1.6 0.1 copy.9
  1.8 0.0 copy-start.1
  1.8 1.4 %copy-done.1 = f32[4,2,384,128]{3,2,1,0:T(8,128)S(1)} copy-done((f32[4,2,384,128]{3,2,1,0:T(8,128)S(1)}, f32[4,2,384,128]{3,2,1,0:T(8,128)}, u32[]{:S(2)}) %copy-start.1) | copy-done | bytes 1572888
  3.2 20.4 %shard_map.77 = f32[4,2,384,128]{3,2,1,0:T(8,128)S(1)} custom-call(f32[384,12]{1,0:T(8,128)S(1)} %bitcast.10, f32[4,2,384,128]{3,2,1,0:T(8,128)S(1)} %copy-done.1), custom_call_target="tpu_custom_call" | custom-call | tf_op jit(solution)/shard_map/pallas_call | solution.py:188
  23.6 0.0 copy-done
  23.6 0.0 copy-start.3
  23.6 0.0 copy-start.2
  23.6 7.2 %fusion.product_ref = f32[512,256]{1,0:T(8,128)S(1)} fusion(f32[3072,256]{1,0:T(8,128)S(1)} %bitcast.8, f32[3072,128]{1,0:T(8,128)} %bitcast.13, f32[3072,128]{1,0:T(8,128)S(1)} %bitcast.6), kind=kOutput, calls=%fused_computation | convolution fusion | flops 2419851264 | bytes 6815744 | tf_op jit(solution)/shard_map/dot_general | solution.py:484
  30.8 20.8 %shard_map.78 = (f32[256,256]{1,0:T(8,128)S(1)}, f32[256,256]{1,0:T(8,128)S(1)}) custom-call(f32[512,256]{1,0:T(8,128)S(1)} %fusion.product_ref), custom_call_target="tpu_custom_call" | custom-call | tf_op jit(solution)/shard_map/pallas_call | solution.py:376
  51.6 0.0 copy-done.3
  51.7 12.5 %shard_map.79 = (f32[256,256]{1,0:T(8,128)S(1)}, f32[256,256]{1,0:T(8,128)S(1)}) custom-call(f32[256,256]{1,0:T(8,128)S(1)} %get-tuple-element.8.gram_ref, f32[256,256]{1,0:T(8,128)S(1)} %get-tuple-element.9.cross_ref, f32[256,256]{1,0:T(8,128)S(1)} %copy-done.3), custom_call_target="tpu_custom_call" | custom-call | tf_op jit(solution)/shard_map/pallas_call | solution.py:419
  64.2 0.0 copy-done.2
  64.2 5.3 %shard_map.80 = (f32[3072,128]{1,0:T(8,128)S(1)}, f32[3072,128]{1,0:T(8,128)}) custom-call(f32[3072,256]{1,0:T(8,128)S(1)} %bitcast.9, f32[3072,128]{1,0:T(8,128)S(1)} %bitcast.7, f32[3072,128]{1,0:T(8,128)S(1)} %bitcast.14, f32[256,256]{1,0:T(8,128)S(1)} %get-tuple-element.10.inv_ref, f32[256,256]{1,0:T(8,128)S(1)} %get-tuple-element.11.mix_ref), custom_call_target="tpu_custom_call" | custom-call | tf_op jit(solution)/shard_map/pallas_call | solution.py:460
  69.4 20.2 %shard_map.81 = f32[4,2,384,128]{3,2,1,0:T(8,128)S(1)} custom-call(f32[384,12]{1,0:T(8,128)S(1)} %bitcast.11, f32[4,2,384,128]{3,2,1,0:T(8,128)S(1)} %bitcast.12), custom_call_target="tpu_custom_call" | custom-call | tf_op jit(solution)/shard_map/pallas_call | solution.py:188
  89.6 1.1 %copy.11 = f32[4,2,384,128]{3,2,1,0:T(8,128)} copy(f32[4,2,384,128]{3,2,1,0:T(8,128)S(1)} %shard_map.81) | data formatting | bytes 3145728
  (1 shorter events, 0.0 us)
Async XLA Ops:
  0.6 23.0 %copy-start = (f32[4,2,384,256]{3,2,1,0:T(8,128)S(1)}, f32[4,2,384,256]{3,2,1,0:T(8,128)}, u32[]{:S(2)}) copy-start(f32[4,2,384,256]{3,2,1,0:T(8,128)} %param.9) | copy-start | bytes 9437188
  1.8 1.4 %copy-start.1 = (f32[4,2,384,128]{3,2,1,0:T(8,128)S(1)}, f32[4,2,384,128]{3,2,1,0:T(8,128)}, u32[]{:S(2)}) copy-start(f32[4,2,384,128]{3,2,1,0:T(8,128)} %value_ref.1) | copy-start | bytes 4718596
  23.6 28.0 %copy-start.3 = (f32[256,256]{1,0:T(8,128)S(1)}, f32[256,256]{1,0:T(8,128)}, u32[]{:S(2)}) copy-start(f32[256,256]{1,0:T(8,128)} %bar_ref.1) | copy-start | bytes 786436
  23.6 40.5 %copy-start.2 = (f32[4,2,384,128]{3,2,1,0:T(8,128)S(1)}, f32[4,2,384,128]{3,2,1,0:T(8,128)}, u32[]{:S(2)}) copy-start(f32[4,2,384,128]{3,2,1,0:T(8,128)} %param.8) | copy-start | bytes 4718596
